TPU v7x, 32 devices: a whole 2x2x4 slice. The times are simulated.
32 devices in a mesh: section: 2 (over core), replica: 4 (over z), shard: 4 (over y, x).
Axes of the slice: x: 2, y: 2, z: 4, core: 2. Of those that a mesh axis runs over, the one named last changes fastest.
Arguments:
- inputs: bfloat16 [4, 2, 1024, 384], P('replica', None, 'shard'), may hold values from -6 to 6
- cotangent: bfloat16 [4, 2, 1024, 384], P('replica', None, 'shard'), may hold values from -6 to 6
- clip_present: int32 [4, 2], P('replica'), may hold values 0 or 1
- qkv_weight: bfloat16 [2, 384, 1152], P('section', 'shard'), may hold values from -0.4375 to 0.4375
- out_weight: bfloat16 [2, 384, 384], P('section', 'shard'), may hold values from -0.875 to 0.875
- up_weight: bfloat16 [2, 384, 1536], P('section', 'shard'), may hold values from -0.3125 to 0.3125
- down_weight: bfloat16 [2, 1536, 384], P('section', 'shard'), may hold values from -0.15625 to 0.15625
- norm_gains: float32 [2, 2, 384], P('section'), may hold values from 0.5 to 1.5
- biases: float32 [2, 6, 384], P('section'), may hold values from -3 to 3
- up_bias: float32 [2, 1536], P('section'), may hold values from -3 to 3
Outputs:
- section_outputs: bfloat16 [2, 4, 2, 1024, 384], P('section', 'replica', None, 'shard')
- input_grads: bfloat16 [2, 4, 2, 1024, 384], P('section', 'replica', None, 'shard')
- qkv_grad: float32 [2, 384, 1152], P('section', ('replica', 'shard'))
- out_grad: float32 [2, 384, 384], P('section', ('replica', 'shard'))
- up_grad: float32 [2, 384, 1536], P('section', ('replica', 'shard'))
- down_grad: float32 [2, 1536, 384], P('section', ('replica', 'shard'))
- gain_grad: float32 [2, 2, 384], P('section', None, ('replica', 'shard'))
- bias_grad: float32 [2, 6, 384], P('section', None, ('replica', 'shard'))
- up_bias_grad: float32 [2, 1536], P('section', ('replica', 'shard'))
All inputs are finite; a program needn't handle non-finite values. No bound on the sum of `clip_present` on one device may be relied on, other than what follows from the above.
Results may differ from a plain program's by a relative error of at most 0.019.
Values may be sent and summed in bfloat16 or wider, within the bound.
No kernel may reach another device: no remote copies, remote signals or barrier semaphores. Data moves between devices by JAX's collectives and lax.ppermute only.
A program may use at most 128 MiB of HBM per device.

v0:
```python
import functools

import jax
import jax.numpy as jnp
from jax import lax
from jax.experimental import pallas as pl
from jax.experimental.pallas import tpu as pltpu
from jax.sharding import PartitionSpec as P

D = 384
HEADS = 6
HEAD_DIM = 64
FF = 1536
PAIR = 2 * HEAD_DIM
HALF = 768
SHARDS = 4
BF = jnp.bfloat16
F32 = jnp.float32
VEC_ROWS = 16
COST = 1000

NT = (((1,), (1,)), ((), ()))
TN = (((0,), (0,)), ((), ()))


def dot(left, right, dims=(((1,), (0,)), ((), ()))):
    return lax.dot_general(left, right, dims, preferred_element_type=F32)


def xor_pass(x, axis, by):
    pairs = [(i, i ^ by) for i in range(lax.axis_size(axis))]
    return lax.ppermute(x, axis, pairs)


def call(kernel, outs, args, name, flops, scalars=1, ties=(), raw=0, scratch=()):
    smem = pl.BlockSpec(memory_space=pltpu.SMEM)
    vmem = pl.BlockSpec(memory_space=pltpu.VMEM)
    apart = pl.BlockSpec(memory_space=pl.ANY)
    size = sum(a.size * a.dtype.itemsize for a in args)
    size += sum(o.size * o.dtype.itemsize for o in outs)
    count = len(args)

    def body(*refs):
        kernel(*refs[:count], *refs[count + len(ties) :])

    return pl.pallas_call(
        body,
        out_shape=outs,
        in_specs=[smem] * scalars
        + [vmem] * (count - scalars - raw)
        + [apart] * (raw + len(ties)),
        out_specs=[vmem] * len(outs),
        scratch_shapes=list(scratch),
        compiler_params=pltpu.CompilerParams(vmem_limit_bytes=20 * 1024 * 1024),
        cost_estimate=pl.CostEstimate(
            flops=flops // COST, bytes_accessed=size // COST, transcendentals=0
        ),
        name=name,
    )(*args, *ties)


def after(arrays, *ties):
    apart = pl.BlockSpec(memory_space=pl.ANY)
    count = len(arrays)
    return pl.pallas_call(
        lambda *refs: None,
        out_shape=[jax.ShapeDtypeStruct(x.shape, x.dtype) for x in arrays],
        in_specs=[apart] * (count + len(ties)),
        out_specs=[apart] * count,
        input_output_aliases={i: i for i in range(count)},
        compiler_params=pltpu.CompilerParams(vmem_limit_bytes=1024 * 1024),
        name="after",
    )(*arrays, *ties)


def sds(shape, dtype):
    return jax.ShapeDtypeStruct(shape, dtype)


def normed(values):
    center = values - jnp.mean(values, axis=-1, keepdims=True)
    spread = jnp.mean(center * center, axis=-1, keepdims=True)
    rstd = lax.rsqrt(spread + 1e-05)
    return center * rstd, rstd


def norm_back(d, xhat, rstd, gain):
    dg = d * gain
    first = jnp.mean(dg, axis=-1, keepdims=True)
    second = jnp.mean(dg * xhat, axis=-1, keepdims=True)
    return rstd * (dg - first - xhat * second)


def col_sum(values):
    return jnp.sum(values, axis=0, keepdims=True)


def half_mask(rows, half):
    lane = lax.broadcasted_iota(jnp.int32, (rows, PAIR), 1)
    return (lane >= HEAD_DIM) if half else (lane < HEAD_DIM)


def held_rows(ids, parts, stepped):
    me, section = ids[0], ids[1]
    for side in range(2):
        half = section ^ side
        by = (0, 1 + half, 2 - half, 3) if stepped else (0, 1, 2, 3)
        for k, part in zip(by, parts[side]):
            yield (me ^ k) * 2 + half, part


def place_rows(ids, full_ref, parts, stepped, first_col):
    width = full_ref.shape[1]
    for place, part in held_rows(ids, parts, stepped):
        rows = part.shape[0]
        at = pl.multiple_of(place * rows, rows)
        full_ref[pl.ds(at, rows), :] = part[:, first_col : first_col + width]


def pack_kernel(ids, out, up, down, stay_ref, swap_ref, sems):
    section = ids[1]
    rows = out.shape[0] // 2
    copies = []

    def move(source, target):
        copy = pltpu.make_async_copy(source, target, sems.at[len(copies)])
        copy.start()
        copies.append(copy)

    for half, ref in ((1 - section, swap_ref), (section, stay_ref)):
        at = pl.ds(pl.multiple_of(half * rows, rows), rows)
        move(out.at[at, :], ref.at[:, :D])
        move(up.at[at, :], ref.at[:, D : D + FF])
        for j in range(4):
            at = pl.ds(pl.multiple_of(half * (4 * rows) + j * rows, rows), rows)
            move(down.at[at, :], ref.at[:, D + FF + j * D : D + FF + (j + 1) * D])
    for copy in copies:
        copy.wait()


def small_kernel(gains, biases, up_b, small_ref):
    bias = up_b[...]
    small_ref[...] = jnp.concatenate(
        [gains[...], biases[...]]
        + [bias[:, j * D : (j + 1) * D] for j in range(4)]
        + [jnp.zeros((4, D), F32)],
        axis=0,
    )


def pick_kernel(ids, stay, got, zero_ref, one_ref):
    first = ids[1] == 0
    here, there = stay[...], got[...]
    zero_ref[...] = jnp.where(first, here, there)
    one_ref[...] = jnp.where(first, there, here)


def outgoing_kernel(ids, pair, block_ref, half_ref):
    section = ids[1]
    low = ids[0] < 2
    here = jnp.where(low, pair[0], pair[1])
    there = jnp.where(low, pair[1], pair[0])
    block_ref[...] = jnp.where(section == 0, here, there)
    cut = half_ref.shape[0]
    half_ref[...] = jnp.where(section == 0, there[:cut], there[cut:])


def arrange_kernel(ids, pair, mine, other, half_mine, half_other, own, core, near, across):
    section = ids[1]
    first = section == 0
    local = jnp.where(ids[0] < 2, pair[0], pair[1])
    beside = jnp.where(first, mine[...], other[...])
    far = jnp.where(first, other[...], mine[...])
    top, bottom = half_mine[...], half_other[...]
    diagonal = jnp.concatenate(
        [jnp.where(first, top, bottom), jnp.where(first, bottom, top)], axis=0
    )
    home = section == ids[0] >> 1
    own[...] = jnp.where(home, local, far)
    core[...] = jnp.where(home, far, local)
    near[...] = jnp.where(home, beside, diagonal)
    across[...] = jnp.where(home, diagonal, beside)


def away_kernel(ids, pair, out_ref):
    out_ref[...] = jnp.where(ids[0] < 2, pair[1], pair[0])


def home_kernel(ids, present, pair, got, out_ref):
    here = jnp.where(ids[0] < 2, pair[0], pair[1])
    value = jnp.where(ids[1] == ids[0] >> 1, here, got[...])
    mask = present[0, ids[0] >> 1].astype(F32)
    out_ref[...] = (value.astype(F32) * mask).astype(BF)


def order_kernel(ids, zero, one, same_ref, swap_ref):
    low = ids[0] < 2
    same_ref[...] = jnp.where(low, zero[...], one[...])
    swap_ref[...] = jnp.where(low, one[...], zero[...])


def clips_kernel(ids, same, swap, out_ref):
    first = ids[1] == 0
    out_ref[0, 0, 0] = jnp.where(first, same[...], swap[...])
    out_ref[0, 0, 1] = jnp.where(first, swap[...], same[...])


def choose_kernel(n, ids, mlp, attn, both, out_ref):
    first = ids[1] == 0
    out_ref[: 2 * n, :] = jnp.where(first, both[: 2 * n, :], mlp[...])
    out_ref[2 * n :, :] = jnp.where(first, both[2 * n : 3 * n, :], attn[:n, :])


def section_sum_kernel(stepped, *refs):
    parts = len(refs) // (6 if stepped else 7)
    outs = refs[3 * parts :]
    per = len(outs) // parts
    for part in range(parts):
        keep, got_one, got_two = refs[3 * part : 3 * part + 3]
        own_ref, *others = outs[per * part : per * part + per]
        sums = [
            keep[e].astype(F32) + (got_one, got_two)[e // 2][e % 2].astype(F32) for e in range(4)
        ]
        own_ref[...] = sums[0]
        if stepped:
            others[0][0] = sums[1].astype(BF)
            others[0][1] = sums[2].astype(BF)
            others[1][...] = sums[3]
        else:
            for ref, total in zip(others, sums[1:]):
                ref[...] = total.astype(BF)


def second_kernel(second, got, out_ref):
    out_ref[...] = (second[...] + got[1].astype(F32)).astype(BF)


def spread_kernel(groups, terms, ids, *refs):
    count = len(groups)
    outs = refs[terms * count :]
    size = len(outs)
    rows = D // SHARDS // size
    me = ids[3]
    base = 0
    for part in range(count):
        total = refs[terms * part][...]
        for ref in refs[terms * part + 1 : terms * part + terms]:
            total = total + (ref[0] if len(ref.shape) == 3 else ref[...]).astype(F32)
        end = base + groups[part] * rows
        tail = total[groups[part] * size * rows :, :]
        if tail.shape[0]:
            for ref in outs:
                ref[end : end + tail.shape[0], :] = tail.astype(ref.dtype)
        for r in range(size):
            block = jnp.concatenate(
                [
                    total[(g * size + r) * rows : (g * size + r + 1) * rows, :]
                    for g in range(groups[part])
                ],
                axis=0,
            )
            for k, ref in enumerate(outs):

                @pl.when(me ^ k == r)
                def _():
                    ref[base:end, :] = block.astype(ref.dtype)

        base = end + tail.shape[0]


def finish_kernel(
    ids, mlp_zero, attn_zero, both_one, got,
    qkv, out, up, down, gain, bias, up_vec,
):
    first = ids[1] == 0

    def sides(zero, one, other):
        own = jnp.where(first, zero, one)
        return jnp.where(first, own, other), jnp.where(first, other, own)

    n = mlp_zero.shape[0] // 2
    low, high = sides(mlp_zero[...], both_one[: 2 * n, :], got[: 2 * n, :])
    up[0, :, :HALF] = low[:n]
    up[0, :, HALF:] = high[:n]
    for t, side in enumerate((low, high)):
        for j in range(2):
            at = (2 * t + j) * n
            down[0, at : at + n, :] = side[n:, j * D : (j + 1) * D]
    low, high = sides(attn_zero[:n, :], both_one[2 * n : 3 * n, :], got[2 * n :, :])
    qkv[0, :, :HALF] = low
    qkv[0, :, HALF:] = high[:, :D]
    out[0] = high[:, D:]
    vec_zero, vec_one = attn_zero[n:, :], both_one[3 * n :, :]
    sums = jnp.where(first, vec_zero, vec_one)

    def taken(values, width):
        length = values.shape[1]
        source = lax.broadcasted_iota(jnp.int32, (length, width), 0)
        target = lax.broadcasted_iota(jnp.int32, (length, width), 1) + ids[2] * width
        spots = jnp.where(source == target, 1.0, 0.0)
        return lax.dot_general(
            values, spots, (((1,), (0,)), ((), ())),
            preferred_element_type=F32, precision=lax.Precision.HIGHEST,
        )

    rows = []
    for r in range(4):
        rows += [sums[r : r + 1, :D], sums[r : r + 1, D:]]
    vec = taken(jnp.concatenate(rows, axis=0), n)
    gain[0] = vec[:2]
    bias[0] = vec[2:]
    both = jnp.concatenate([sums[4:5], sums[5:6]], axis=1)
    up_vec[...] = taken(jnp.broadcast_to(both, (8, FF)), 4 * n)[:1]


def attend_kernel(
    layer, ids, x0, x1, x2, x3, w0, w1, w2, w3, o0, o1, o2, o3, small,
    w_ref, xhat_ref, q_ref, k_ref, v_ref, lse_ref, mixed_ref,
):
    me = ids[0]
    rows = x0.shape[0]
    own_layer = ids[1] == layer
    for k, (own, other) in enumerate(((w0, o0), (w1, o1), (w2, o2), (w3, o3))):
        count = own.shape[0]
        at = pl.multiple_of((me ^ k) * count, count)
        w_ref[pl.ds(at, count), :] = jnp.where(own_layer, own[...], other[...])
    gains, biases = small[0:2, :], small[2:8, :]
    gain, shift = gains[0:1, :], biases[0:1, :]
    for r, x in enumerate((x0, x1, x2, x3)):
        xhat, unused = normed(x[...].astype(F32))
        xhat_ref[r * rows : (r + 1) * rows, :] = xhat.astype(BF)
        a = (xhat * gain + shift).astype(BF)
        if r == 0:
            q = (dot(a, w_ref[:, :D]) + biases[1:2, :]).astype(BF)
            q_ref[...] = (q.astype(F32) * (HEAD_DIM ** (-0.5))).astype(BF)
        k_ref[r * rows : (r + 1) * rows, :] = dot(a, w_ref[:, D : 2 * D]).astype(BF)
        v_ref[r * rows : (r + 1) * rows, :] = (
            dot(a, w_ref[:, 2 * D :]) + biases[2:3, :]
        ).astype(BF)

    def one_pair(pair, carry):
        cols = pl.ds(pl.multiple_of(pair * PAIR, PAIR), PAIR)
        k_pair = k_ref[:, cols]
        v_t = v_ref[:, cols].T
        q_pair = q_ref[:, cols].astype(F32)
        mixed_t = []
        for half in range(2):
            qm = jnp.where(half_mask(rows, half), q_pair, 0.0).astype(BF)
            s = dot(k_pair, qm, NT)
            top = jnp.max(s, axis=0, keepdims=True)
            e = jnp.exp(s - top)
            total = jnp.sum(e, axis=0, keepdims=True)
            lse_ref[pl.ds(2 * pair + half, 1), :] = top + jnp.log(total)
            o = dot(v_t[half * HEAD_DIM : (half + 1) * HEAD_DIM, :], e.astype(BF))
            mixed_t.append(o * (1.0 / total))
        mixed_ref[:, cols] = jnp.concatenate(mixed_t, axis=0).T.astype(BF)
        return carry

    lax.fori_loop(0, HEADS // 2, one_pair, 0)


def mlp_kernel(stepped, ids, present, x0, mixed, *refs):
    out_ref, resid_ref, z_ref, slope_ref, wo_ref, w1_ref, w2_ref = refs[-7:]
    small = refs[-8]
    count = (len(refs) - 8) // 2
    parts = [refs[:count], refs[count : 2 * count]]
    if stepped:
        parts = [(own, got, pair.at[0], pair.at[1]) for own, got, pair in parts]
    place_rows(ids, wo_ref, parts, stepped, 0)
    place_rows(ids, w1_ref, parts, stepped, D)
    for place, part in held_rows(ids, parts, stepped):
        rows = part.shape[0]
        for j in range(4):
            at = pl.multiple_of((place * 4 + j) * rows, rows)
            left = D + FF + j * D
            w2_ref[pl.ds(at, rows), :] = part[:, left : left + D]
    gains, biases = small[0:2, :], small[2:8, :]
    up_b = jnp.concatenate([small[8 + j : 9 + j, :] for j in range(4)], axis=1)
    resid = x0[...].astype(F32) + (dot(mixed[...], wo_ref[...]) + biases[3:4, :])
    resid_ref[...] = resid
    xhat, unused = normed(resid)
    c = (xhat * gains[1:2, :] + biases[4:5, :]).astype(BF)
    upper = dot(c, w1_ref[...]) + up_b
    phi = 0.5 * (1.0 + lax.erf(upper * (2.0 ** -0.5)))
    z = (upper * phi).astype(BF)
    z_ref[...] = z
    bell = jnp.exp(-0.5 * upper * upper) * 0.3989422804014327
    slope_ref[...] = (phi + upper * bell).astype(BF)
    out = resid + (dot(z, w2_ref[...]) + biases[5:6, :])
    out_ref[...] = (out * present[0, ids[0] >> 1].astype(F32)).astype(BF)


def mlp_back_kernel(
    gout, z, slope, resid, wo, w1, w2, small,
    dresid_ref, ga_ref, du_ref, c_ref, dmixed_ref, vec_ref, upvec_ref,
):
    gains, biases = small[0:2, :], small[2:8, :]
    gm = gout[...]
    dz = dot(gm, w2[...], NT)
    du = (dz * slope[...].astype(F32)).astype(BF)
    du_ref[...] = du
    dc = dot(du, w1[...], NT)
    xhat, rstd = normed(resid[...])
    gain = gains[1:2, :]
    c_ref[...] = (xhat * gain + biases[4:5, :]).astype(BF)
    g_full = gm.astype(F32)
    dresid = g_full + norm_back(dc, xhat, rstd, gain)
    dresid_ref[...] = dresid
    ga = dresid.astype(BF)
    ga_ref[...] = ga
    dmixed_ref[...] = dot(ga, wo[...], NT).astype(BF)
    vec_ref[...] = jnp.concatenate(
        [
            col_sum(dc * xhat),
            col_sum(dc),
            col_sum(ga.astype(F32)),
            col_sum(g_full),
            jnp.zeros((4, D), F32),
        ],
        axis=0,
    )
    upvec_ref[...] = col_sum(du.astype(F32))


def attend_back_kernel(
    q_ref, k_ref, v_ref, lse, mixed, dmixed, xhat_ref, w_ref,
    own_ref, near_ref, swap_ref, dq_ref, dkv_ref, vec_ref,
):
    rows = q_ref.shape[0]

    def one_pair(pair, carry):
        cols = pl.ds(pl.multiple_of(pair * PAIR, PAIR), PAIR)
        k_pair, v_pair = k_ref[:, cols], v_ref[:, cols]
        k_t = k_pair.T
        q_pair = q_ref[:, cols].astype(F32)
        do_pair = dmixed[:, cols].astype(F32)
        prod_t = (mixed[:, cols].astype(F32) * do_pair).T
        dq_t, ps, dss, qms, doms = [], [], [], [], []
        for half in range(2):
            keep = half_mask(rows, half)
            qm = jnp.where(keep, q_pair, 0.0).astype(BF)
            dom = jnp.where(keep, do_pair, 0.0).astype(BF)
            p = jnp.exp(dot(k_pair, qm, NT) - lse[pl.ds(2 * pair + half, 1), :])
            dp = dot(v_pair, dom, NT)
            delta = col_sum(prod_t[half * HEAD_DIM : (half + 1) * HEAD_DIM, :])
            ds = (p * (dp - delta)).astype(BF)
            dq_t.append(
                dot(k_t[half * HEAD_DIM : (half + 1) * HEAD_DIM, :], ds) * (HEAD_DIM ** (-0.5))
            )
            ps.append(p.astype(BF))
            dss.append(ds)
            qms.append(qm)
            doms.append(dom)
        dkv_ref[:, cols] = dot(
            jnp.concatenate(dss, axis=1), jnp.concatenate(qms, axis=0)
        ).astype(BF)
        dkv_ref[:, pl.ds(pl.multiple_of(D + pair * PAIR, PAIR), PAIR)] = dot(
            jnp.concatenate(ps, axis=1), jnp.concatenate(doms, axis=0)
        ).astype(BF)
        dq_ref[:, cols] = jnp.concatenate(dq_t, axis=0).T.astype(BF)
        return carry

    lax.fori_loop(0, HEADS // 2, one_pair, 0)
    dq = dq_ref[...]
    gain_sum = jnp.zeros((1, D), F32)
    shift_sum = jnp.zeros((1, D), F32)
    outs = (own_ref, swap_ref.at[0], near_ref, swap_ref.at[1])
    for r, da_ref in enumerate(outs):
        at = slice(r * rows, (r + 1) * rows)
        da = dot(dkv_ref[at, :], w_ref[:, D:], NT)
        if r == 0:
            da = da + dot(dq, w_ref[:, :D], NT)
        gain_sum = gain_sum + col_sum(da * xhat_ref[at, :].astype(F32))
        shift_sum = shift_sum + col_sum(da)
        da_ref[...] = da.astype(da_ref.dtype)
    vec_ref[...] = jnp.concatenate(
        [
            gain_sum,
            shift_sum,
            col_sum(dq.astype(F32)),
            col_sum(dkv_ref[:, D:].astype(F32)),
            jnp.zeros((4, D), F32),
        ],
        axis=0,
    )


def norm_back_kernel(da_own, da_core, da_near, x0, dresid, small, out_ref):
    da = da_own[...] + da_core[0].astype(F32) + da_near[...].astype(F32)
    xhat, rstd = normed(x0[...].astype(F32))
    out_ref[...] = (dresid[...] + norm_back(da, xhat, rstd, small[0:1, :])).astype(BF)


def regroup(grad, s, replicas):
    rows = grad.shape[0] // (replicas * SHARDS)
    pieces = []
    for r in range(replicas):
        start = (r * SHARDS + s) * rows
        pieces.append(grad[start : start + rows, :])
    return pieces


def slot_of(ids, s, side):
    by = ids[0] ^ s
    if side is None:
        return by
    turned = jnp.where(side == 0, by, ((by & 1) << 1) | (by >> 1))
    return turned ^ (turned >> 1)


def put(refs, slot, at, block):
    @pl.when(slot < 2)
    def _():
        refs[0][slot, at, :] = block

    @pl.when(slot >= 2)
    def _():
        refs[1][slot - 2, at, :] = block


def grad_kernel(
    replicas, layer, ids, c, du, z, gm, xhat, dq, dkv, mixed, ga, small, vec_one, vec_two,
    upvec, *outs,
):
    section = ids[1]
    first = section == 0
    base = D // SHARDS
    start_of = 2 * base if layer == 1 else 0
    side = section if layer == 1 else None

    def store(refs, s, at, own, other):
        keep_ref, *send_refs = refs
        keep_ref[slot_of(ids, s, side), at, :] = own.astype(BF)
        away = None if side is None else 1 - side
        put(send_refs, slot_of(ids, s, away), at, other.astype(BF))

    def store_halves(refs, grad, at):
        left, right = grad[:, :HALF], grad[:, HALF:]
        own = jnp.where(first, left, right)
        other = jnp.where(first, right, left)
        for s in range(SHARDS):
            blocks = [
                jnp.concatenate(regroup(half, s, replicas), axis=0) for half in (own, other)
            ]
            store(refs, s, at, *blocks)

    store_halves(outs[:3], dot(c[...], du[...], TN), slice(0, base))
    grad = dot(z[...], gm[...], TN)
    rows = FF // (replicas * SHARDS)
    sub = rows // 4
    for s in range(SHARDS):
        sides = ([], [])
        for r in range(replicas):
            start = (r * SHARDS + s) * rows
            parts = [grad[start + j * sub : start + (j + 1) * sub, :] for j in range(4)]
            sides[0].append(jnp.concatenate(parts[:2], axis=1))
            sides[1].append(jnp.concatenate(parts[2:], axis=1))
        low, high = (jnp.concatenate(side, axis=0) for side in sides)
        own, other = jnp.where(first, low, high), jnp.where(first, high, low)
        store(outs[:3], s, slice(base, 2 * base), own, other)
    count = dq.shape[0]
    a = (xhat[...].astype(F32) * small[0:1, :] + small[2:3, :]).astype(BF)
    grad = jnp.concatenate(
        [
            dot(a[:count, :], dq[...], TN),
            dot(a, dkv[...], TN),
            dot(mixed[...], ga[...], TN),
        ],
        axis=1,
    )
    store_halves(outs[-3:], grad, slice(start_of, start_of + base))
    one, two, up = vec_one[...], vec_two[...], upvec[...]

    def wide(left, right):
        return jnp.concatenate([left, right], axis=1)

    vec = jnp.concatenate(
        [
            wide(one[0:1], two[0:1]),
            wide(one[1:2], one[2:3]),
            wide(one[3:4], two[2:3]),
            wide(two[1:2], two[3:4]),
            up[:, :HALF],
            up[:, HALF:],
            jnp.zeros((VEC_ROWS - 6, HALF), F32),
        ],
        axis=0,
    ).astype(BF)
    at = slice(start_of + base, start_of + base + VEC_ROWS)
    for s in range(SHARDS):
        outs[-3][s, at, :] = vec
        outs[-2 + s // 2][s % 2, at, :] = vec


def shard_spread(block):
    return [block] + [xor_pass(block, "shard", k) for k in (1, 2, 3)]


def stack_kernel(one, two, out_ref):
    out_ref[0] = one[...]
    out_ref[1] = two[...]


def shard_steps(block):
    return block, lax.ppermute(block, ("section", "shard"), split_pairs(1, 2))


def shard_steps_end(block, got, tie):
    (pair,) = call(
        stack_kernel,
        [sds((2,) + block.shape, BF)],
        [block, got],
        "stack",
        1_000_000,
        scalars=0,
        ties=(tie,),
    )
    return [block, got, lax.ppermute(pair, ("section", "shard"), split_pairs(2, 1))]


def both_cores(parts):
    return [*parts, *(xor_pass(part, "section", 1) for part in parts)]


def clip_frames(own):
    near = xor_pass(own, "shard", 1)
    return [own, xor_pass(own, "section", 1), near, xor_pass(near, "section", 1)]


def first_frames(ids, pair, weight):
    rows = sds(pair.shape[1:], BF)
    half = sds((pair.shape[1] // 2, pair.shape[2]), BF)
    block, part = call(outgoing_kernel, [rows, half], [ids, pair], "outgoing", 1_000_000)
    mine = lax.ppermute(block, ("section", "shard"), split_pairs(1, 2))
    half_mine = xor_pass(part, "shard", 3)
    parts = shard_spread(weight)
    mine, half_mine = after([mine, half_mine], *parts[1:])
    other, half_other = (xor_pass(got, "section", 1) for got in (mine, half_mine))
    frames = call(
        arrange_kernel,
        [rows] * 4,
        [ids, pair, mine, other, half_mine, half_other],
        "arrange",
        1_000_000,
    )
    return block, list(frames), both_cores(parts)


def to_clip(ids, present, pair):
    count = lax.axis_size("shard")
    pairs = [((i >> 1) * count + i, (i >> 1) * count + (i ^ 2)) for i in range(count)]
    rows = sds(pair.shape[1:], BF)
    (away,) = call(away_kernel, [rows], [ids, pair], "away", 1_000_000)
    got = lax.ppermute(away, ("section", "shard"), pairs)
    (home,) = call(
        home_kernel,
        [rows],
        [ids, present, pair, got],
        "home",
        1_000_000,
        scalars=2,
    )
    return home


def from_clip(ids, pair):
    count = lax.axis_size("shard")

    def pairs(flip):
        out = []
        for sec in range(2):
            for i in range(count):
                clip, low = i >> 1, i & 1
                out.append((sec * count + i, (clip ^ flip) * count + sec * 2 + low))
        return out

    both = ("section", "shard")
    rows = sds(pair[0].shape, BF)
    same, swap = call(order_kernel, [rows, rows], [ids, *pair], "order", 1_000_000)
    return lax.ppermute(same, both, pairs(0)), lax.ppermute(swap, both, pairs(1))


def clips_of(ids, same, swap):
    out = sds((1, 1, 2) + same.shape, BF)
    return call(clips_kernel, [out], [ids, same, swap], "clips", 1_000_000)[0]


def section_sum(parts, stepped, ties):
    args, outs = [], []
    for keep, *send in parts:
        rows = keep.shape[1]
        args += [keep, *(xor_pass(part, "section", 1) for part in send)]
        outs.append(sds((rows, HALF), F32))
        if stepped:
            outs += [sds((2, rows, HALF), BF), sds((rows, HALF), F32)]
        else:
            outs += [sds((rows, HALF), BF)] * 3
    sums = call(
        functools.partial(section_sum_kernel, stepped),
        outs,
        args,
        "section_sum",
        1_000_000,
        scalars=0,
        ties=ties,
    )
    per = len(outs) // len(parts)
    return [sums[i * per : (i + 1) * per] for i in range(len(parts))]


def split_pairs(low, high):
    count = lax.axis_size("shard")
    return [(i, i ^ low) for i in range(count)] + [
        (count + i, count + (i ^ high)) for i in range(count)
    ]


def shard_first(first_out, low):
    return lax.ppermute(first_out, ("section", "shard"), split_pairs(low, 3 - low))


def shard_second(second_out, got, low, ties):
    (message,) = call(
        second_kernel,
        [sds(second_out.shape, BF)],
        [second_out, got],
        "second",
        1_000_000,
        scalars=0,
        ties=ties,
    )
    return lax.ppermute(message, ("section", "shard"), split_pairs(3 - low, low))


def replica_sum(ids, parts, ties):
    size = lax.axis_size("replica")
    rows = D // SHARDS // size
    groups = [(part[1].shape[0] - part[0]) // (D // SHARDS) for part in parts]
    if size > SHARDS:
        pieces = []
        for (fixed, *terms), count in zip(parts, groups):
            summed = sum((t[0] if t.ndim == 3 else t).astype(F32) for t in terms)
            blocks = summed[: count * size * rows].reshape(count, size, rows, HALF)
            blocks = blocks.transpose(1, 0, 2, 3).reshape(size, count * rows, HALF)
            mine = lax.psum_scatter(blocks.astype(BF), "replica", scatter_dimension=0)
            pieces.append(mine.astype(F32))
            if fixed:
                pieces.append(lax.psum(summed[count * size * rows :], "replica"))
        return jnp.concatenate(pieces, axis=0)
    count = sum(groups) * rows + sum(part[0] for part in parts)
    own, *messages = call(
        functools.partial(spread_kernel, groups, len(parts[0]) - 1),
        [sds((count, HALF), F32)] + [sds((count, HALF), BF)] * (size - 1),
        [ids] + [array for part in parts for array in part[1:]],
        "spread",
        1_000_000,
        ties=ties,
    )
    for k, message in enumerate(messages):
        own = own + xor_pass(message, "replica", k + 1).astype(F32)
    return own


def local(
    inputs,
    cotangent,
    clip_present,
    qkv_weight,
    out_weight,
    up_weight,
    down_weight,
    norm_gains,
    biases,
    up_bias,
):
    section = lax.axis_index("section")
    shard = lax.axis_index("shard")
    replica = lax.axis_index("replica")
    replicas = lax.axis_size("replica")
    first = section == 0
    rows = inputs.shape[2]
    place = replica * SHARDS + shard
    ids = jnp.stack([shard, section, place, replica]).astype(jnp.int32)
    own_rows = D // SHARDS

    arrived, frames, qkv_part = first_frames(ids, inputs[0], qkv_weight[0])

    (late,) = after([cotangent[0]], arrived)
    gout_last = to_clip(ids, clip_present, late)

    half_rows = own_rows // 2
    packed = sds((half_rows, 9 * D), BF)
    stay, swap = call(
        pack_kernel,
        [packed, packed],
        [ids, out_weight[0], up_weight[0], down_weight[0]],
        "pack",
        1_000_000,
        raw=3,
        ties=(arrived,),
        scratch=[pltpu.SemaphoreType.DMA((12,))],
    )
    got = xor_pass(swap, "section", 1)
    (small,) = call(
        small_kernel,
        [sds((16, D), F32)],
        [norm_gains[0], biases[0], up_bias[0][None]],
        "small",
        1_000_000,
        scalars=0,
        ties=(arrived,),
    )
    other_small = xor_pass(small, "section", 1)
    both = sds((16, D), F32)
    small_layers = call(
        pick_kernel, [both, both], [ids, small, other_small], "small_pick", 1_000_000
    )
    rest_zero, rest_one = call(
        pick_kernel, [packed, packed], [ids, stay, got], "pick", 1_000_000,
        ties=(*qkv_part[1:4], gout_last),
    )
    rest_part = shard_spread(rest_zero)

    whole = SHARDS * rows
    saved = []
    outs = []
    for layer in range(2):
        small = small_layers[layer]
        w_qkv, xhat, q, k, v, lse, mixed = call(
            functools.partial(attend_kernel, layer),
            [
                sds((D, 3 * D), BF),
                sds((whole, D), BF),
                sds((rows, D), BF),
                sds((whole, D), BF),
                sds((whole, D), BF),
                sds((8, rows), F32),
                sds((rows, D), BF),
            ],
            [ids, *frames, *qkv_part, small],
            "attend",
            4_000_000_000,
        )
        if layer == 0:
            last_parts = shard_steps(after([rest_one], mixed)[0])
            rest_part = both_cores([rest_part[0], *after(rest_part[1:], mixed)])
        else:
            rest_part = both_cores([last_parts[0], *after(last_parts[1:], mixed)])
        out, resid, z, slope, w_out, w_up, w_down = call(
            functools.partial(mlp_kernel, layer == 1),
            [
                sds((rows, D), BF),
                sds((rows, D), F32),
                sds((rows, FF), BF),
                sds((rows, FF), BF),
                sds((D, D), BF),
                sds((D, FF), BF),
                sds((FF, D), BF),
            ],
            [ids, clip_present, frames[0], mixed, *rest_part, small],
            "mlp",
            2_000_000_000,
            scalars=2,
        )
        saved.append(
            (frames[0], w_qkv, xhat, q, k, v, lse, mixed, resid, z, slope, w_out, w_up, w_down)
        )
        outs.append(out)
        if layer == 0:
            frames = clip_frames(out)
            last_parts = shard_steps_end(*last_parts, frames[2])

    outs_back = from_clip(ids, outs)
    gout = gout_last
    shares = [None, None]
    grads = [None, None]
    before = ()
    for layer in (1, 0):
        small = small_layers[layer]
        x0, w_qkv, xhat, q, k, v, lse, mixed, resid, z, slope, w_out, w_up, w_down = saved[layer]
        dresid, ga, du, c, dmixed, vec_two, upvec = call(
            mlp_back_kernel,
            [
                sds((rows, D), F32),
                sds((rows, D), BF),
                sds((rows, FF), BF),
                sds((rows, D), BF),
                sds((rows, D), BF),
                sds((8, D), F32),
                sds((1, FF), F32),
            ],
            [gout, z, slope, resid, w_out, w_up, w_down, small],
            "mlp_back",
            2_000_000_000,
            scalars=0,
        )
        da_own, da_near, da_swap, dq, dkv, vec_one = call(
            attend_back_kernel,
            [
                sds((rows, D), F32),
                sds((rows, D), F32),
                sds((2, rows, D), BF),
                sds((rows, D), BF),
                sds((whole, 2 * D), BF),
                sds((8, D), F32),
            ],
            [q, k, v, lse, mixed, dmixed, xhat, w_qkv],
            "attend_back",
            8_000_000_000,
            scalars=0,
            ties=before,
        )
        got = xor_pass(da_swap, "section", 1)
        near = (da_near + got[1].astype(F32)).astype(BF)
        back = xor_pass(near, "shard", 1)
        counts = [3 * own_rows + VEC_ROWS]
        if layer == 0:
            counts = [2 * own_rows, own_rows + VEC_ROWS]
        shapes = []
        for count in counts:
            shapes += [sds((SHARDS, count, HALF), BF)] + [sds((2, count, HALF), BF)] * 2
        parts = call(
            functools.partial(grad_kernel, replicas, layer),
            shapes,
            [ids, c, du, z, gout, xhat, dq, dkv, mixed, ga, small, vec_one, vec_two, upvec],
            "grad",
            4_000_000_000,
            ties=(near,) if layer == 1 else (),
        )
        if layer == 1:
            keep, *send = parts
            parts = [(keep, *after(send, back, *outs_back))]
            ((own, first_out, second_out),) = section_sum(parts, True, ())
            before = (first_out,)
        else:
            parts = section_sum((parts[:3], parts[3:]), False, (back, late))
        (gin,) = call(
            norm_back_kernel,
            [sds((rows, D), BF)],
            [da_own, got, back, x0, dresid, small],
            "norm_back",
            100_000_000,
            scalars=0,
        )
        grads[layer] = gin
        gout = gin
        if layer == 1:
            got = shard_first(first_out, 1)
            late = shard_second(second_out, got, 1, ())
            shares[1] = replica_sum(ids, [(VEC_ROWS, own, got, late)], ())
        else:
            sums = []
            for (own, *messages), fixed in zip(parts, (0, VEC_ROWS)):
                gots = [xor_pass(m, "shard", k + 1) for k, m in enumerate(messages)]
                sums.append((fixed, own, *gots))
            shares[0] = [
                replica_sum(ids, sums[:1], (shares[1],)), replica_sum(ids, sums[1:], ())
            ]

    outputs_local = clips_of(ids, *outs_back)
    grads_local = clips_of(ids, *from_clip(ids, grads))
    n = own_rows // replicas
    (away,) = call(
        functools.partial(choose_kernel, n),
        [sds((3 * n, HALF), F32)],
        [ids, *shares[0], shares[1]],
        "choose",
        1_000_000,
        ties=(outputs_local, grads_local),
    )
    got = xor_pass(away, "section", 1)
    qkv_grad, out_grad, up_grad, down_grad, gain, bias, up_vec = call(
        finish_kernel,
        [
            sds((1, n, 3 * D), F32),
            sds((1, n, D), F32),
            sds((1, n, FF), F32),
            sds((1, 4 * n, D), F32),
            sds((1, 2, n), F32),
            sds((1, 6, n), F32),
            sds((1, 4 * n), F32),
        ],
        [ids, *shares[0], shares[1], got],
        "finish",
        1_000_000,
    )
    return (
        outputs_local,
        grads_local,
        qkv_grad,
        out_grad,
        up_grad,
        down_grad,
        gain,
        bias,
        up_vec,
    )


def solution(mesh):
    return jax.shard_map(
        local,
        mesh=mesh,
        in_specs=(
            P("replica", None, "shard", None),
            P("replica", None, "shard", None),
            P("replica", None),
            P("section", "shard", None),
            P("section", "shard", None),
            P("section", "shard", None),
            P("section", "shard", None),
            P("section", None, None),
            P("section", None, None),
            P("section", None),
        ),
        out_specs=(
            P("section", "replica", None, "shard", None),
            P("section", "replica", None, "shard", None),
            P("section", ("replica", "shard"), None),
            P("section", ("replica", "shard"), None),
            P("section", ("replica", "shard"), None),
            P("section", ("replica", "shard"), None),
            P("section", None, ("replica", "shard")),
            P("section", None, ("replica", "shard")),
            P("section", ("replica", "shard")),
        ),
        check_vma=False,
    )
```

profile of v0, /device:TPU:0, one launch (start us, length us, event | category | flops | bytes accessed | tf_op | source)
XLA Modules:
  0.0 165.6 jit_solution(10247693761425861801)
XLA Ops:
  3.4 3.0 %collective-permute-start = (bf16[256,384]{1,0:T(8,128)(2,1)S(1)}, bf16[256,384]{1,0:T(8,128)(2,1)S(1)}, u32[]{:S(2)}, u32[]{:S(2)}) collective-permute-start(bf16[256,384]{1,0:T(8,128)(2,1)S(1)} %get-tuple-element.127.refs_3_.refs_4_.refs_1_), channel_id=1, source_target_pairs={{0,1},{1,0},{2,3},{3,2},{16,18},{17,19},{18,16},{19,17},{4,5},{5,4... | collective-permute-start | bytes 589832 | tf_op jit(solution)/shard_map/ppermute | solution.py:634
  12.7 5.8 %collective-permute-done.1.refs_1_ = bf16[128,384]{1,0:T(8,128)(2,1)S(1)} collective-permute-done((bf16[128,384]{1,0:T(8,128)(2,1)S(1)}, bf16[128,384]{1,0:T(8,128)(2,1)S(1)}, u32[]{:S(2)}, u32[]{:S(2)}) %collective-permute-start.1) | collective-permute-done | bytes 98336 | tf_op jit(solution)/shard_map/ppermute | solution.py:32
  20.6 2.4 %collective-permute-start.13 = (bf16[256,384]{1,0:T(8,128)(2,1)S(1)}, bf16[256,384]{1,0:T(8,128)(2,1)S(1)}, u32[]{:S(2)}, u32[]{:S(2)}) collective-permute-start(bf16[256,384]{1,0:T(8,128)(2,1)S(1)} %away.1), channel_id=1, source_target_pairs={{0,2},{1,3},{18,16},{19,17},{4,6},{5,7},{22,20},{23,21},{8,10},{9,... | collective-permute-start | bytes 589832 | tf_op jit(solution)/shard_map/ppermute | solution.py:654
  28.0 2.0 %collective-permute-start.16 = (bf16[48,3456]{1,0:T(8,128)(2,1)S(1)}, bf16[48,3456]{1,0:T(8,128)(2,1)S(1)}, u32[]{:S(2)}, u32[]{:S(2)}) collective-permute-start(bf16[48,3456]{1,0:T(8,128)(2,1)S(1)} %get-tuple-element.139.refs_4_), channel_id=1, source_target_pairs={{0,3},{1,2},{2,1},{3,0},{4,7},{5,6},{6,5},{7,4},{8,11},{9,10},{10,... | collective-permute-start | bytes 995336 | tf_op jit(solution)/shard_map/ppermute | solution.py:32
  34.1 7.2 %attend.2 = (bf16[384,1152]{1,0:T(8,128)(2,1)S(1)}, bf16[1024,384]{1,0:T(8,128)(2,1)S(1)}, bf16[256,384]{1,0:T(8,128)(2,1)S(1)}, bf16[1024,384]{1,0:T(8,128)(2,1...) custom-call(s32[4]{0:T(128)S(1)} %pad_add_fusion.refs_0_, ...), custom_call_target="tpu_custom_call" | custom-call | flops 4000000 | bytes 6225 | tf_op jit(solution)/shard_map/attend/pallas_call | solution.py:46
  41.3 4.5 %collective-permute-done.15.refs_1_ = bf16[48,3456]{1,0:T(8,128)(2,1)S(1)} collective-permute-done((bf16[48,3456]{1,0:T(8,128)(2,1)S(1)}, bf16[48,3456]{1,0:T(8,128)(2,1)S(1)}, u32[]{:S(2)}, u32[]{:S(2)}) %collective-permute-start.15) | collective-permute-done | bytes 331808 | tf_op jit(solution)/shard_map/ppermute | solution.py:32
  49.5 2.5 %mlp.2 = (bf16[256,384]{1,0:T(8,128)(2,1)S(1)}, f32[256,384]{1,0:T(8,128)S(1)}, bf16[256,1536]{1,0:T(8,128)(2,1)S(1)}, bf16[256,1536]{1,0:T(8,128)(2,1)S(1)}, bf...) custom-call(s32[4]{0:T(128)S(1)} %pad_add_fusion.refs_0_, ...), custom_call_target="tpu_custom_call" | custom-call | flops 2000000 | bytes 7888 | tf_op jit(solution)/shard_map/mlp/pallas_call | solution.py:46
  52.3 2.3 %collective-permute-done.24.refs_1_.refs_0_ = bf16[48,3456]{1,0:T(8,128)(2,1)S(1)} collective-permute-done((bf16[48,3456]{1,0:T(8,128)(2,1)S(1)}, bf16[48,3456]{1,0:T(8,128)(2,1)S(1)}, u32[]{:S(2)}, u32[]{:S(2)}) %collective-permute-start.24) | collective-permute-done | bytes 331808 | tf_op jit(solution)/shard_map/ppermute | solution.py:605
  54.5 4.4 %collective-permute-done.22.refs_3_.refs_2_ = bf16[256,384]{1,0:T(8,128)(2,1)S(1)} collective-permute-done((bf16[256,384]{1,0:T(8,128)(2,1)S(1)}, bf16[256,384]{1,0:T(8,128)(2,1)S(1)}, u32[]{:S(2)}, u32[]{:S(2)}) %collective-permute-start.22) | collective-permute-done | bytes 196640 | tf_op jit(solution)/shard_map/ppermute | solution.py:32
  61.4 7.0 %attend.3 = (bf16[384,1152]{1,0:T(8,128)(2,1)S(1)}, bf16[1024,384]{1,0:T(8,128)(2,1)S(1)}, bf16[256,384]{1,0:T(8,128)(2,1)S(1)}, bf16[1024,384]{1,0:T(8,128)(2,1...) custom-call(s32[4]{0:T(128)S(1)} %pad_add_fusion.refs_0_, ...), custom_call_target="tpu_custom_call" | custom-call | flops 4000000 | bytes 6225 | tf_op jit(solution)/shard_map/attend/pallas_call | solution.py:46
  70.3 2.1 %collective-permute-done.26.refs_7_ = bf16[48,3456]{1,0:T(8,128)(2,1)S(1)} collective-permute-done((bf16[48,3456]{1,0:T(8,128)(2,1)S(1)}, bf16[48,3456]{1,0:T(8,128)(2,1)S(1)}, u32[]{:S(2)}, u32[]{:S(2)}) %collective-permute-start.26) | collective-permute-done | bytes 331808 | tf_op jit(solution)/shard_map/ppermute | solution.py:32
  72.8 2.5 %mlp.3 = (bf16[256,384]{1,0:T(8,128)(2,1)S(1)}, f32[256,384]{1,0:T(8,128)S(1)}, bf16[256,1536]{1,0:T(8,128)(2,1)S(1)}, bf16[256,1536]{1,0:T(8,128)(2,1)S(1)}, bf...) custom-call(s32[4]{0:T(128)S(1)} %pad_add_fusion.refs_0_, ...), custom_call_target="tpu_custom_call" | custom-call | flops 2000000 | bytes 7888 | tf_op jit(solution)/shard_map/mlp/pallas_call | solution.py:46
  76.8 6.0 %attend_back.2 = (f32[256,384]{1,0:T(8,128)S(1)}, f32[256,384]{1,0:T(8,128)S(1)}, bf16[2,256,384]{2,1,0:T(8,128)(2,1)S(1)}, bf16[256,384]{1,0:T(8,128)(2,1)S(1)}...) custom-call(bf16[256,384]{1,0:T(8,128)(2,1)S(1)} %get-tuple-element.156.refs_0_, ...), custom_call_target="tpu_custom_call" | custom-call | flops 8000000 | bytes 6803 | tf_op jit(solution)/shard_map/attend_back/pallas_call | solution.py:46
  84.5 2.0 %collective-permute-start.30 = (bf16[256,384]{1,0:T(8,128)(2,1)S(1)}, bf16[256,384]{1,0:T(8,128)(2,1)S(1)}, u32[]{:S(2)}, u32[]{:S(2)}) collective-permute-start(bf16[256,384]{1,0:T(8,128)(2,1)S(1)} %get-tuple-element.151), channel_id=1, source_target_pairs={{0,16},{1,17},{2,0},{3,1},{16,18},{17,19},{18,2},{19,3},{4,20},{5,... | collective-permute-start | bytes 589832 | tf_op jit(solution)/shard_map/ppermute | solution.py:680
  87.4 3.4 %grad.2 = (bf16[4,304,768]{2,1,0:T(8,128)(2,1)S(1)}, bf16[2,304,768]{2,1,0:T(8,128)(2,1)S(1)}, bf16[2,304,768]{2,1,0:T(8,128)(2,1)S(1)}) custom-call(s32[4]{0:T(128)S(1)} %pad_add_fusion.refs_0_, bf16[256,384]{1,0:T(8,128)(2,1)S(1)} %get-tuple-element.182.refs_1_, bf16[256,1536]{1,0:T(8,128)(2,1)S(1)} %get-tuple-element.183.refs_2_, ...), custom_call_target="tpu_custom_call" | custom-call | flops 4000000 | bytes 8706 | tf_op jit(solution)/shard_map/grad/pallas_call | solution.py:46
  90.9 2.4 %collective-permute-done.30.refs_2_.refs_4_ = bf16[256,384]{1,0:T(8,128)(2,1)S(1)} collective-permute-done((bf16[256,384]{1,0:T(8,128)(2,1)S(1)}, bf16[256,384]{1,0:T(8,128)(2,1)S(1)}, u32[]{:S(2)}, u32[]{:S(2)}) %collective-permute-start.30) | collective-permute-done | bytes 196640 | tf_op jit(solution)/shard_map/ppermute | solution.py:680
  94.0 2.0 %collective-permute-done.33.refs_1_ = bf16[2,304,768]{2,1,0:T(8,128)(2,1)S(1)} collective-permute-done((bf16[2,304,768]{2,1,0:T(8,128)(2,1)S(1)}, bf16[2,304,768]{2,1,0:T(8,128)(2,1)S(1)}, u32[]{:S(2)}, u32[]{:S(2)}) %collective-permute-start.33) | collective-permute-done | bytes 933920 | tf_op jit(solution)/shard_map/ppermute | solution.py:32
  100.4 5.9 %attend_back.3 = (f32[256,384]{1,0:T(8,128)S(1)}, f32[256,384]{1,0:T(8,128)S(1)}, bf16[2,256,384]{2,1,0:T(8,128)(2,1)S(1)}, bf16[256,384]{1,0:T(8,128)(2,1)S(1)}...) custom-call(bf16[256,384]{1,0:T(8,128)(2,1)S(1)} %get-tuple-element.152.refs_0_, ...), custom_call_target="tpu_custom_call" | custom-call | flops 8000000 | bytes 6803 | tf_op jit(solution)/shard_map/attend_back/pallas_call | solution.py:46
  109.5 3.4 %grad.3 = (bf16[4,192,768]{2,1,0:T(8,128)(2,1)S(1)}, bf16[2,192,768]{2,1,0:T(8,128)(2,1)S(1)}, bf16[2,192,768]{2,1,0:T(8,128)(2,1)S(1)}, bf16[4,112,768]{2,1,0:T...) custom-call(s32[4]{0:T(128)S(1)} %pad_add_fusion.refs_0_, ...), custom_call_target="tpu_custom_call" | custom-call | flops 4000000 | bytes 8706 | tf_op jit(solution)/shard_map/grad/pallas_call | solution.py:46
  113.5 1.8 %collective-permute-start.44 = (bf16[304,768]{1,0:T(8,128)(2,1)S(1)}, bf16[304,768]{1,0:T(8,128)(2,1)S(1)}, u32[]{:S(2)}, u32[]{:S(2)}) collective-permute-start(bf16[304,768]{1,0:T(8,128)(2,1)S(1)} %second.1), channel_id=1, source_target_pairs={{0,2},{1,3},{2,0},{3,1},{16,17},{17,16},{18,19},{19,18},{4,6},{5,7... | collective-permute-start | bytes 1400840 | tf_op jit(solution)/shard_map/ppermute | solution.py:732
  117.7 2.7 %collective-permute-start.38 = (bf16[256,384]{1,0:T(8,128)(2,1)S(1)}, bf16[256,384]{1,0:T(8,128)(2,1)S(1)}, u32[]{:S(2)}, u32[]{:S(2)}) collective-permute-start(bf16[256,384]{1,0:T(8,128)(2,1)S(1)} %get-tuple-element.201), channel_id=1, source_target_pairs={{0,16},{1,17},{2,0},{3,1},{16,18},{17,19},{18,2},{19,3},{4,20},{5,... | collective-permute-start | bytes 589832 | tf_op jit(solution)/shard_map/ppermute | solution.py:680
  120.3 1.8 %collective-permute-done.44.refs_7_.refs_3_ = bf16[304,768]{1,0:T(8,128)(2,1)S(1)} collective-permute-done((bf16[304,768]{1,0:T(8,128)(2,1)S(1)}, bf16[304,768]{1,0:T(8,128)(2,1)S(1)}, u32[]{:S(2)}, u32[]{:S(2)}) %collective-permute-start.44) | collective-permute-done | bytes 466976 | tf_op jit(solution)/shard_map/ppermute | solution.py:732
  127.5 2.4 %collective-permute-start.55 = (bf16[112,768]{1,0:T(8,128)(2,1)S(1)}, bf16[112,768]{1,0:T(8,128)(2,1)S(1)}, u32[]{:S(2)}, u32[]{:S(2)}) collective-permute-start(bf16[112,768]{1,0:T(8,128)(2,1)S(1)} %get-tuple-element.232), channel_id=1, source_target_pairs={{0,2},{1,3},{2,0},{3,1},{4,6},{5,7},{6,4},{7,5},{8,10},{9,11},{10,... | collective-permute-start | bytes 516104 | tf_op jit(solution)/shard_map/ppermute | solution.py:32
  130.9 2.6 %collective-permute-start.49 = (bf16[88,768]{1,0:T(8,128)(2,1)S(1)}, bf16[88,768]{1,0:T(8,128)(2,1)S(1)}, u32[]{:S(2)}, u32[]{:S(2)}) collective-permute-start(bf16[88,768]{1,0:T(8,128)(2,1)S(1)} %get-tuple-element.224), channel_id=1, source_target_pairs={{0,8},{4,12},{8,0},{12,4},{1,9},{5,13},{9,1},{13,5},{2,10},{6,14},... | collective-permute-start | bytes 405512 | tf_op jit(solution)/shard_map/ppermute | solution.py:32
  134.9 2.4 %collective-permute-start.46 = (bf16[192,768]{1,0:T(8,128)(2,1)S(1)}, bf16[192,768]{1,0:T(8,128)(2,1)S(1)}, u32[]{:S(2)}, u32[]{:S(2)}) collective-permute-start(bf16[192,768]{1,0:T(8,128)(2,1)S(1)} %get-tuple-element.219), channel_id=1, source_target_pairs={{0,2},{1,3},{2,0},{3,1},{4,6},{5,7},{6,4},{7,5},{8,10},{9,11},{10,... | collective-permute-start | bytes 884744 | tf_op jit(solution)/shard_map/ppermute | solution.py:32
  137.3 2.2 %collective-permute-done.56.refs_4_ = bf16[112,768]{1,0:T(8,128)(2,1)S(1)} collective-permute-done((bf16[112,768]{1,0:T(8,128)(2,1)S(1)}, bf16[112,768]{1,0:T(8,128)(2,1)S(1)}, u32[]{:S(2)}, u32[]{:S(2)}) %collective-permute-start.56) | collective-permute-done | bytes 172064 | tf_op jit(solution)/shard_map/ppermute | solution.py:32
  145.5 2.6 %collective-permute-start.58 = (bf16[40,768]{1,0:T(8,128)(2,1)S(1)}, bf16[40,768]{1,0:T(8,128)(2,1)S(1)}, u32[]{:S(2)}, u32[]{:S(2)}) collective-permute-start(bf16[40,768]{1,0:T(8,128)(2,1)S(1)} %get-tuple-element.236), channel_id=1, source_target_pairs={{0,8},{4,12},{8,0},{12,4},{1,9},{5,13},{9,1},{13,5},{2,10},{6,14},... | collective-permute-start | bytes 184328 | tf_op jit(solution)/shard_map/ppermute | solution.py:32
  148.3 1.9 %collective-permute-done.46.refs_3_ = bf16[192,768]{1,0:T(8,128)(2,1)S(1)} collective-permute-done((bf16[192,768]{1,0:T(8,128)(2,1)S(1)}, bf16[192,768]{1,0:T(8,128)(2,1)S(1)}, u32[]{:S(2)}, u32[]{:S(2)}) %collective-permute-start.46) | collective-permute-done | bytes 294944 | tf_op jit(solution)/shard_map/ppermute | solution.py:32
  152.2 2.5 %collective-permute-start.52 = (bf16[48,768]{1,0:T(8,128)(2,1)S(1)}, bf16[48,768]{1,0:T(8,128)(2,1)S(1)}, u32[]{:S(2)}, u32[]{:S(2)}) collective-permute-start(bf16[48,768]{1,0:T(8,128)(2,1)S(1)} %get-tuple-element.228), channel_id=1, source_target_pairs={{0,8},{4,12},{8,0},{12,4},{1,9},{5,13},{9,1},{13,5},{2,10},{6,14},... | collective-permute-start | bytes 221192 | tf_op jit(solution)/shard_map/ppermute | solution.py:32
  155.6 3.2 %collective-permute-done.52 = bf16[48,768]{1,0:T(8,128)(2,1)S(1)} collective-permute-done((bf16[48,768]{1,0:T(8,128)(2,1)S(1)}, bf16[48,768]{1,0:T(8,128)(2,1)S(1)}, u32[]{:S(2)}, u32[]{:S(2)}) %collective-permute-start.52) | collective-permute-done | bytes 73760 | tf_op jit(solution)/shard_map/ppermute | solution.py:32
  158.8 2.1 %collective-permute-done.53 = bf16[48,768]{1,0:T(8,128)(2,1)S(1)} collective-permute-done((bf16[48,768]{1,0:T(8,128)(2,1)S(1)}, bf16[48,768]{1,0:T(8,128)(2,1)S(1)}, u32[]{:S(2)}, u32[]{:S(2)}) %collective-permute-start.53) | collective-permute-done | bytes 73760 | tf_op jit(solution)/shard_map/ppermute | solution.py:32
  163.1 1.9 %finish.1 = (f32[1,24,1152]{2,1,0:T(8,128)}, f32[1,24,384]{2,1,0:T(8,128)}, f32[1,24,1536]{2,1,0:T(8,128)}, f32[1,96,384]{2,1,0:T(8,128)}, f32[1,2,24]{2,1,0:T(2...) custom-call(s32[4]{0:T(128)S(1)} %pad_add_fusion.refs_0_, f32[48,768]{1,0:T(8,128)S(1)} %convert_add_fusion.3.refs_1_, ...), custom_call_target="tpu_custom_call" | custom-call | flops 1000 | bytes 1205 | tf_op jit(solution)/shard_map/finish/pallas_call | solution.py:46
  (162 shorter events, 63.6 us)
Async XLA Ops:
  3.4 17.2 %collective-permute-start = (bf16[256,384]{1,0:T(8,128)(2,1)S(1)}, bf16[256,384]{1,0:T(8,128)(2,1)S(1)}, u32[]{:S(2)}, u32[]{:S(2)}) collective-permute-start(bf16[256,384]{1,0:T(8,128)(2,1)S(1)} %get-tuple-element.127.refs_3_.refs_4_.refs_1_), channel_id=1, source_target_pairs={{0,1},{1,0},{2,3},{3,2},{16,18},{17,19},{18,16},{19,17},{4,5},{5,4... | collective-permute-start | bytes 589832 | tf_op jit(solution)/shard_map/ppermute | solution.py:634
  6.4 16.6 %collective-permute-start.4 = (bf16[96,1152]{1,0:T(8,128)(2,1)S(1)}, bf16[96,1152]{1,0:T(8,128)(2,1)S(1)}, u32[]{:S(2)}, u32[]{:S(2)}) collective-permute-start(bf16[96,1152]{1,0:T(8,128)(2,1)S(1)} %bitcast.27), channel_id=1, source_target_pairs={{0,3},{1,2},{2,1},{3,0},{4,7},{5,6},{6,5},{7,4},{8,11},{9,10},{10,... | collective-permute-start | bytes 663560 | tf_op jit(solution)/shard_map/ppermute | solution.py:32
  7.9 10.6 %collective-permute-start.1 = (bf16[128,384]{1,0:T(8,128)(2,1)S(1)}, bf16[128,384]{1,0:T(8,128)(2,1)S(1)}, u32[]{:S(2)}, u32[]{:S(2)}) collective-permute-start(bf16[128,384]{1,0:T(8,128)(2,1)S(1)} %get-tuple-element.128), channel_id=1, source_target_pairs={{0,3},{1,2},{2,1},{3,0},{4,7},{5,6},{6,5},{7,4},{8,11},{9,10},{10,... | collective-permute-start | bytes 294920 | tf_op jit(solution)/shard_map/ppermute | solution.py:32
  11.1 15.2 %collective-permute-start.12 = (bf16[48,3456]{1,0:T(8,128)(2,1)S(1)}, bf16[48,3456]{1,0:T(8,128)(2,1)S(1)}, u32[]{:S(2)}, u32[]{:S(2)}) collective-permute-start(bf16[48,3456]{1,0:T(8,128)(2,1)S(1)} %get-tuple-element.138), channel_id=1, source_target_pairs={{0,16},{16,0},{1,17},{17,1},{2,18},{18,2},{3,19},{19,3},{4,20},{20... | collective-permute-start | bytes 995336 | tf_op jit(solution)/shard_map/ppermute | solution.py:32
  11.1 12.0 %collective-permute-start.3 = (bf16[96,1152]{1,0:T(8,128)(2,1)S(1)}, bf16[96,1152]{1,0:T(8,128)(2,1)S(1)}, u32[]{:S(2)}, u32[]{:S(2)}) collective-permute-start(bf16[96,1152]{1,0:T(8,128)(2,1)S(1)} %bitcast.28), channel_id=1, source_target_pairs={{0,2},{1,3},{2,0},{3,1},{4,6},{5,7},{6,4},{7,5},{8,10},{9,11},{10,... | collective-permute-start | bytes 663560 | tf_op jit(solution)/shard_map/ppermute | solution.py:32
  23.2 9.0 %collective-permute-start.10 = (bf16[96,1152]{1,0:T(8,128)(2,1)S(1)}, bf16[96,1152]{1,0:T(8,128)(2,1)S(1)}, u32[]{:S(2)}, u32[]{:S(2)}) collective-permute-start(bf16[96,1152]{1,0:T(8,128)(2,1)S(1)} %collective-permute-done.4.refs_4_.refs_8_.refs_5_), channel_id=1, source_target_pairs={{0,16},{16,0},{1,17},{17,1},{2,18},{18,2},{3,19},{19,3},{4,20},{20... | collective-permute-start | bytes 663560 | tf_op jit(solution)/shard_map/ppermute | solution.py:32
  28.0 13.3 %collective-permute-start.16 = (bf16[48,3456]{1,0:T(8,128)(2,1)S(1)}, bf16[48,3456]{1,0:T(8,128)(2,1)S(1)}, u32[]{:S(2)}, u32[]{:S(2)}) collective-permute-start(bf16[48,3456]{1,0:T(8,128)(2,1)S(1)} %get-tuple-element.139.refs_4_), channel_id=1, source_target_pairs={{0,3},{1,2},{2,1},{3,0},{4,7},{5,6},{6,5},{7,4},{8,11},{9,10},{10,... | collective-permute-start | bytes 995336 | tf_op jit(solution)/shard_map/ppermute | solution.py:32
  30.0 15.8 %collective-permute-start.15 = (bf16[48,3456]{1,0:T(8,128)(2,1)S(1)}, bf16[48,3456]{1,0:T(8,128)(2,1)S(1)}, u32[]{:S(2)}, u32[]{:S(2)}) collective-permute-start(bf16[48,3456]{1,0:T(8,128)(2,1)S(1)} %get-tuple-element.139.refs_4_), channel_id=1, source_target_pairs={{0,2},{1,3},{2,0},{3,1},{4,6},{5,7},{6,4},{7,5},{8,10},{9,11},{10,... | collective-permute-start | bytes 995336 | tf_op jit(solution)/shard_map/ppermute | solution.py:32
  30.7 16.2 %collective-permute-start.14 = (bf16[48,3456]{1,0:T(8,128)(2,1)S(1)}, bf16[48,3456]{1,0:T(8,128)(2,1)S(1)}, u32[]{:S(2)}, u32[]{:S(2)}) collective-permute-start(bf16[48,3456]{1,0:T(8,128)(2,1)S(1)} %get-tuple-element.139.refs_4_), channel_id=1, source_target_pairs={{0,1},{1,0},{2,3},{3,2},{4,5},{5,4},{6,7},{7,6},{8,9},{9,8},{10,11... | collective-permute-start | bytes 995336 | tf_op jit(solution)/shard_map/ppermute | solution.py:32
  34.0 13.8 %collective-permute-start.17 = (bf16[48,3456]{1,0:T(8,128)(2,1)S(1)}, bf16[48,3456]{1,0:T(8,128)(2,1)S(1)}, u32[]{:S(2)}, u32[]{:S(2)}) collective-permute-start(bf16[48,3456]{1,0:T(8,128)(2,1)S(1)} %get-tuple-element.139.refs_4_), channel_id=1, source_target_pairs={{0,16},{16,0},{1,17},{17,1},{2,18},{18,2},{3,19},{19,3},{4,20},{20... | collective-permute-start | bytes 995336 | tf_op jit(solution)/shard_map/ppermute | solution.py:32
  47.4 7.1 %collective-permute-start.24 = (bf16[48,3456]{1,0:T(8,128)(2,1)S(1)}, bf16[48,3456]{1,0:T(8,128)(2,1)S(1)}, u32[]{:S(2)}, u32[]{:S(2)}) collective-permute-start(bf16[48,3456]{1,0:T(8,128)(2,1)S(1)} %after.9.refs_0_.refs_4_), channel_id=1, source_target_pairs={{0,1},{1,0},{2,3},{3,2},{16,18},{17,19},{18,16},{19,17},{4,5},{5,4... | collective-permute-start | bytes 995336 | tf_op jit(solution)/shard_map/ppermute | solution.py:605
  59.0 10.7 %collective-permute-start.25 = (bf16[2,48,3456]{2,1,0:T(8,128)(2,1)S(1)}, bf16[2,48,3456]{2,1,0:T(8,128)(2,1)S(1)}, u32[]{:S(2)}, u32[]{:S(2)}) collective-permute-start(bf16[2,48,3456]{2,1,0:T(8,128)(2,1)S(1)} %stack.21), channel_id=1, source_target_pairs={{0,2},{1,3},{2,0},{3,1},{16,17},{17,16},{18,19},{19,18},{4,6},{5,7... | collective-permute-start | bytes 1990664 | tf_op jit(solution)/shard_map/ppermute | solution.py:618
  83.6 7.3 %collective-permute-start.29 = (bf16[256,384]{1,0:T(8,128)(2,1)S(1)}, bf16[256,384]{1,0:T(8,128)(2,1)S(1)}, u32[]{:S(2)}, u32[]{:S(2)}) collective-permute-start(bf16[256,384]{1,0:T(8,128)(2,1)S(1)} %get-tuple-element.150), channel_id=1, source_target_pairs={{0,0},{1,1},{2,16},{3,17},{16,2},{17,3},{18,18},{19,19},{4,4},{5,5... | collective-permute-start | bytes 589832 | tf_op jit(solution)/shard_map/ppermute | solution.py:680
  84.5 8.7 %collective-permute-start.30 = (bf16[256,384]{1,0:T(8,128)(2,1)S(1)}, bf16[256,384]{1,0:T(8,128)(2,1)S(1)}, u32[]{:S(2)}, u32[]{:S(2)}) collective-permute-start(bf16[256,384]{1,0:T(8,128)(2,1)S(1)} %get-tuple-element.151), channel_id=1, source_target_pairs={{0,16},{1,17},{2,0},{3,1},{16,18},{17,19},{18,2},{19,3},{4,20},{5,... | collective-permute-start | bytes 589832 | tf_op jit(solution)/shard_map/ppermute | solution.py:680
  97.7 15.7 %collective-permute-start.43 = (bf16[2,304,768]{2,1,0:T(8,128)(2,1)S(1)}, bf16[2,304,768]{2,1,0:T(8,128)(2,1)S(1)}, u32[]{:S(2)}, u32[]{:S(2)}) collective-permute-start(bf16[2,304,768]{2,1,0:T(8,128)(2,1)S(1)} %get-tuple-element.195.refs_8_), channel_id=1, source_target_pairs={{0,1},{1,0},{2,3},{3,2},{16,18},{17,19},{18,16},{19,17},{4,5},{5,4... | collective-permute-start | bytes 2801672 | tf_op jit(solution)/shard_map/ppermute | solution.py:719
  108.6 7.2 %collective-permute-start.36 = (bf16[256,384]{1,0:T(8,128)(2,1)S(1)}, bf16[256,384]{1,0:T(8,128)(2,1)S(1)}, u32[]{:S(2)}, u32[]{:S(2)}) collective-permute-start(bf16[256,384]{1,0:T(8,128)(2,1)S(1)} %fusion), channel_id=1, source_target_pairs={{0,1},{1,0},{2,3},{3,2},{4,5},{5,4},{6,7},{7,6},{8,9},{9,8},{10,11... | collective-permute-start | bytes 589832 | tf_op jit(solution)/shard_map/ppermute | solution.py:32
  112.9 7.5 %collective-permute-start.39 = (bf16[2,192,768]{2,1,0:T(8,128)(2,1)S(1)}, bf16[2,192,768]{2,1,0:T(8,128)(2,1)S(1)}, u32[]{:S(2)}, u32[]{:S(2)}) collective-permute-start(bf16[2,192,768]{2,1,0:T(8,128)(2,1)S(1)} %get-tuple-element.211), channel_id=1, source_target_pairs={{0,16},{16,0},{1,17},{17,1},{2,18},{18,2},{3,19},{19,3},{4,20},{20... | collective-permute-start | bytes 1769480 | tf_op jit(solution)/shard_map/ppermute | solution.py:32
  112.9 7.4 %collective-permute-start.40 = (bf16[2,192,768]{2,1,0:T(8,128)(2,1)S(1)}, bf16[2,192,768]{2,1,0:T(8,128)(2,1)S(1)}, u32[]{:S(2)}, u32[]{:S(2)}) collective-permute-start(bf16[2,192,768]{2,1,0:T(8,128)(2,1)S(1)} %get-tuple-element.212), channel_id=1, source_target_pairs={{0,16},{16,0},{1,17},{17,1},{2,18},{18,2},{3,19},{19,3},{4,20},{20... | collective-permute-start | bytes 1769480 | tf_op jit(solution)/shard_map/ppermute | solution.py:32
  113.5 8.6 %collective-permute-start.44 = (bf16[304,768]{1,0:T(8,128)(2,1)S(1)}, bf16[304,768]{1,0:T(8,128)(2,1)S(1)}, u32[]{:S(2)}, u32[]{:S(2)}) collective-permute-start(bf16[304,768]{1,0:T(8,128)(2,1)S(1)} %second.1), channel_id=1, source_target_pairs={{0,2},{1,3},{2,0},{3,1},{16,17},{17,16},{18,19},{19,18},{4,6},{5,7... | collective-permute-start | bytes 1400840 | tf_op jit(solution)/shard_map/ppermute | solution.py:732
  117.0 10.5 %collective-permute-start.37 = (bf16[256,384]{1,0:T(8,128)(2,1)S(1)}, bf16[256,384]{1,0:T(8,128)(2,1)S(1)}, u32[]{:S(2)}, u32[]{:S(2)}) collective-permute-start(bf16[256,384]{1,0:T(8,128)(2,1)S(1)} %get-tuple-element.200), channel_id=1, source_target_pairs={{0,0},{1,1},{2,16},{3,17},{16,2},{17,3},{18,18},{19,19},{4,4},{5,5... | collective-permute-start | bytes 589832 | tf_op jit(solution)/shard_map/ppermute | solution.py:680
  117.7 12.3 %collective-permute-start.38 = (bf16[256,384]{1,0:T(8,128)(2,1)S(1)}, bf16[256,384]{1,0:T(8,128)(2,1)S(1)}, u32[]{:S(2)}, u32[]{:S(2)}) collective-permute-start(bf16[256,384]{1,0:T(8,128)(2,1)S(1)} %get-tuple-element.201), channel_id=1, source_target_pairs={{0,16},{1,17},{2,0},{3,1},{16,18},{17,19},{18,2},{19,3},{4,20},{5,... | collective-permute-start | bytes 589832 | tf_op jit(solution)/shard_map/ppermute | solution.py:680
  122.6 10.9 %collective-permute-start.54 = (bf16[112,768]{1,0:T(8,128)(2,1)S(1)}, bf16[112,768]{1,0:T(8,128)(2,1)S(1)}, u32[]{:S(2)}, u32[]{:S(2)}) collective-permute-start(bf16[112,768]{1,0:T(8,128)(2,1)S(1)} %get-tuple-element.231), channel_id=1, source_target_pairs={{0,1},{1,0},{2,3},{3,2},{4,5},{5,4},{6,7},{7,6},{8,9},{9,8},{10,11... | collective-permute-start | bytes 516104 | tf_op jit(solution)/shard_map/ppermute | solution.py:32
  123.9 24.2 %collective-permute-start.45 = (bf16[192,768]{1,0:T(8,128)(2,1)S(1)}, bf16[192,768]{1,0:T(8,128)(2,1)S(1)}, u32[]{:S(2)}, u32[]{:S(2)}) collective-permute-start(bf16[192,768]{1,0:T(8,128)(2,1)S(1)} %get-tuple-element.218), channel_id=1, source_target_pairs={{0,1},{1,0},{2,3},{3,2},{4,5},{5,4},{6,7},{7,6},{8,9},{9,8},{10,11... | collective-permute-start | bytes 884744 | tf_op jit(solution)/shard_map/ppermute | solution.py:32
  127.5 7.4 %collective-permute-start.55 = (bf16[112,768]{1,0:T(8,128)(2,1)S(1)}, bf16[112,768]{1,0:T(8,128)(2,1)S(1)}, u32[]{:S(2)}, u32[]{:S(2)}) collective-permute-start(bf16[112,768]{1,0:T(8,128)(2,1)S(1)} %get-tuple-element.232), channel_id=1, source_target_pairs={{0,2},{1,3},{2,0},{3,1},{4,6},{5,7},{6,4},{7,5},{8,10},{9,11},{10,... | collective-permute-start | bytes 516104 | tf_op jit(solution)/shard_map/ppermute | solution.py:32
  129.9 9.5 %collective-permute-start.56 = (bf16[112,768]{1,0:T(8,128)(2,1)S(1)}, bf16[112,768]{1,0:T(8,128)(2,1)S(1)}, u32[]{:S(2)}, u32[]{:S(2)}) collective-permute-start(bf16[112,768]{1,0:T(8,128)(2,1)S(1)} %get-tuple-element.233), channel_id=1, source_target_pairs={{0,3},{1,2},{2,1},{3,0},{4,7},{5,6},{6,5},{7,4},{8,11},{9,10},{10,... | collective-permute-start | bytes 516104 | tf_op jit(solution)/shard_map/ppermute | solution.py:32
  130.9 12.9 %collective-permute-start.49 = (bf16[88,768]{1,0:T(8,128)(2,1)S(1)}, bf16[88,768]{1,0:T(8,128)(2,1)S(1)}, u32[]{:S(2)}, u32[]{:S(2)}) collective-permute-start(bf16[88,768]{1,0:T(8,128)(2,1)S(1)} %get-tuple-element.224), channel_id=1, source_target_pairs={{0,8},{4,12},{8,0},{12,4},{1,9},{5,13},{9,1},{13,5},{2,10},{6,14},... | collective-permute-start | bytes 405512 | tf_op jit(solution)/shard_map/ppermute | solution.py:32
  133.5 12.0 %collective-permute-start.50 = (bf16[88,768]{1,0:T(8,128)(2,1)S(1)}, bf16[88,768]{1,0:T(8,128)(2,1)S(1)}, u32[]{:S(2)}, u32[]{:S(2)}) collective-permute-start(bf16[88,768]{1,0:T(8,128)(2,1)S(1)} %get-tuple-element.225), channel_id=1, source_target_pairs={{0,12},{4,8},{8,4},{12,0},{1,13},{5,9},{9,5},{13,1},{2,14},{6,10},... | collective-permute-start | bytes 405512 | tf_op jit(solution)/shard_map/ppermute | solution.py:32
  134.9 15.4 %collective-permute-start.46 = (bf16[192,768]{1,0:T(8,128)(2,1)S(1)}, bf16[192,768]{1,0:T(8,128)(2,1)S(1)}, u32[]{:S(2)}, u32[]{:S(2)}) collective-permute-start(bf16[192,768]{1,0:T(8,128)(2,1)S(1)} %get-tuple-element.219), channel_id=1, source_target_pairs={{0,2},{1,3},{2,0},{3,1},{4,6},{5,7},{6,4},{7,5},{8,10},{9,11},{10,... | collective-permute-start | bytes 884744 | tf_op jit(solution)/shard_map/ppermute | solution.py:32
  139.5 10.8 %collective-permute-start.47 = (bf16[192,768]{1,0:T(8,128)(2,1)S(1)}, bf16[192,768]{1,0:T(8,128)(2,1)S(1)}, u32[]{:S(2)}, u32[]{:S(2)}) collective-permute-start(bf16[192,768]{1,0:T(8,128)(2,1)S(1)} %get-tuple-element.220), channel_id=1, source_target_pairs={{0,3},{1,2},{2,1},{3,0},{4,7},{5,6},{6,5},{7,4},{8,11},{9,10},{10,... | collective-permute-start | bytes 884744 | tf_op jit(solution)/shard_map/ppermute | solution.py:32
  143.8 11.0 %collective-permute-start.57 = (bf16[40,768]{1,0:T(8,128)(2,1)S(1)}, bf16[40,768]{1,0:T(8,128)(2,1)S(1)}, u32[]{:S(2)}, u32[]{:S(2)}) collective-permute-start(bf16[40,768]{1,0:T(8,128)(2,1)S(1)} %get-tuple-element.235), channel_id=1, source_target_pairs={{0,4},{4,0},{8,12},{12,8},{1,5},{5,1},{9,13},{13,9},{2,6},{6,2},{1... | collective-permute-start | bytes 184328 | tf_op jit(solution)/shard_map/ppermute | solution.py:32
  145.5 10.0 %collective-permute-start.58 = (bf16[40,768]{1,0:T(8,128)(2,1)S(1)}, bf16[40,768]{1,0:T(8,128)(2,1)S(1)}, u32[]{:S(2)}, u32[]{:S(2)}) collective-permute-start(bf16[40,768]{1,0:T(8,128)(2,1)S(1)} %get-tuple-element.236), channel_id=1, source_target_pairs={{0,8},{4,12},{8,0},{12,4},{1,9},{5,13},{9,1},{13,5},{2,10},{6,14},... | collective-permute-start | bytes 184328 | tf_op jit(solution)/shard_map/ppermute | solution.py:32
  148.1 7.4 %collective-permute-start.59 = (bf16[40,768]{1,0:T(8,128)(2,1)S(1)}, bf16[40,768]{1,0:T(8,128)(2,1)S(1)}, u32[]{:S(2)}, u32[]{:S(2)}) collective-permute-start(bf16[40,768]{1,0:T(8,128)(2,1)S(1)} %get-tuple-element.237), channel_id=1, source_target_pairs={{0,12},{4,8},{8,4},{12,0},{1,13},{5,9},{9,5},{13,1},{2,14},{6,10},... | collective-permute-start | bytes 184328 | tf_op jit(solution)/shard_map/ppermute | solution.py:32
  (41 other events, 185.8 us)
where the time goes:
time: 166 us
  Pallas kernels  55.9 us (34%)
  starting transfers between devices  55.8 us (34%)
  waiting for transfers between devices  48.9 us (29%)
  local copies, waits for them, and re-layouts  3.58 us (2%)
    pallas_call x33, Pallas kernels, call(): pl.pallas_call(body, out_shape=outs, in_specs=[smem] * scalars + [vmem] *...  55.9 us
    ppermute x51, starting transfers between devices, xor_pass(): return lax.ppermute(x, axis, pairs)  40.5 us
    ppermute x51, waiting for transfers between devices, xor_pass(): return lax.ppermute(x, axis, pairs)  39.3 us
    ppermute x2, starting transfers between devices, from_clip(): lax.ppermute(swap, both, pairs(1))  4.64 us
    unnamed x27, local copies, waits for them, and re-layouts  3.58 us
  transfers between devices with their start and end apart: 61, of which 30 were waited for; matrix products, arithmetic and copies ran while one was open for 0% of the time, Pallas kernels for 26%

commit v1 on v0

--- a/solution.py
+++ b/solution.py
@@ -18,6 +18,7 @@
 F32 = jnp.float32
 VEC_ROWS = 16
 COST = 1000
+LARGEST_SUM = 1e30
 
 NT = (((1,), (1,)), ((), ()))
 TN = (((0,), (0,)), ((), ()))
@@ -155,22 +156,25 @@
     one_ref[...] = jnp.where(first, there, here)
 
 
-def outgoing_kernel(ids, pair, block_ref, half_ref):
+def outgoing_kernel(ids, pair, gouts, block_ref, half_ref):
     section = ids[1]
     low = ids[0] < 2
     here = jnp.where(low, pair[0], pair[1])
     there = jnp.where(low, pair[1], pair[0])
-    block_ref[...] = jnp.where(section == 0, here, there)
+    block_ref[0] = jnp.where(section == 0, here, there)
+    block_ref[1] = jnp.where(low, gouts[1], gouts[0])
     cut = half_ref.shape[0]
     half_ref[...] = jnp.where(section == 0, there[:cut], there[cut:])
 
 
-def arrange_kernel(ids, pair, mine, other, half_mine, half_other, own, core, near, across):
+def arrange_kernel(
+    ids, present, pair, gouts, mine, other, half_mine, half_other, own, core, near, across, gout
+):
     section = ids[1]
     first = section == 0
     local = jnp.where(ids[0] < 2, pair[0], pair[1])
-    beside = jnp.where(first, mine[...], other[...])
-    far = jnp.where(first, other[...], mine[...])
+    beside = jnp.where(first, mine[0], other[0])
+    far = jnp.where(first, other[0], mine[0])
     top, bottom = half_mine[...], half_other[...]
     diagonal = jnp.concatenate(
         [jnp.where(first, top, bottom), jnp.where(first, bottom, top)], axis=0
@@ -180,17 +184,10 @@
     core[...] = jnp.where(home, far, local)
     near[...] = jnp.where(home, beside, diagonal)
     across[...] = jnp.where(home, diagonal, beside)
-
-
-def away_kernel(ids, pair, out_ref):
-    out_ref[...] = jnp.where(ids[0] < 2, pair[1], pair[0])
-
-
-def home_kernel(ids, present, pair, got, out_ref):
-    here = jnp.where(ids[0] < 2, pair[0], pair[1])
-    value = jnp.where(ids[1] == ids[0] >> 1, here, got[...])
     mask = present[0, ids[0] >> 1].astype(F32)
-    out_ref[...] = (value.astype(F32) * mask).astype(BF)
+    far = jnp.where(first, other[1], mine[1])
+    local = jnp.where(ids[0] < 2, gouts[0], gouts[1])
+    gout[...] = (jnp.where(home, local, far).astype(F32) * mask).astype(BF)
 
 
 def order_kernel(ids, zero, one, same_ref, swap_ref):
@@ -295,13 +292,8 @@
 
     def taken(values, width):
         length = values.shape[1]
-        source = lax.broadcasted_iota(jnp.int32, (length, width), 0)
-        target = lax.broadcasted_iota(jnp.int32, (length, width), 1) + ids[2] * width
-        spots = jnp.where(source == target, 1.0, 0.0)
-        return lax.dot_general(
-            values, spots, (((1,), (0,)), ((), ())),
-            preferred_element_type=F32, precision=lax.Precision.HIGHEST,
-        )
+        turn = lax.rem(length - ids[2] * width, length)
+        return pltpu.roll(values, turn, 1)[:, :width]
 
     rows = []
     for r in range(4):
@@ -333,12 +325,11 @@
         if r == 0:
             q = (dot(a, w_ref[:, :D]) + biases[1:2, :]).astype(BF)
             q_ref[...] = (q.astype(F32) * (HEAD_DIM ** (-0.5))).astype(BF)
-        k_ref[r * rows : (r + 1) * rows, :] = dot(a, w_ref[:, D : 2 * D]).astype(BF)
-        v_ref[r * rows : (r + 1) * rows, :] = (
-            dot(a, w_ref[:, 2 * D :]) + biases[2:3, :]
-        ).astype(BF)
-
-    def one_pair(pair, carry):
+        kv = dot(a, w_ref[:, D:])
+        k_ref[r * rows : (r + 1) * rows, :] = kv[:, :D].astype(BF)
+        v_ref[r * rows : (r + 1) * rows, :] = (kv[:, D:] + biases[2:3, :]).astype(BF)
+
+    def one_pair(sample, pair, worst):
         cols = pl.ds(pl.multiple_of(pair * PAIR, PAIR), PAIR)
         k_pair = k_ref[:, cols]
         v_t = v_ref[:, cols].T
@@ -347,16 +338,25 @@
         for half in range(2):
             qm = jnp.where(half_mask(rows, half), q_pair, 0.0).astype(BF)
             s = dot(k_pair, qm, NT)
-            top = jnp.max(s, axis=0, keepdims=True)
+            top = jnp.max(s[:sample], axis=0, keepdims=True)
             e = jnp.exp(s - top)
             total = jnp.sum(e, axis=0, keepdims=True)
+            worst = jnp.maximum(worst, total)
             lse_ref[pl.ds(2 * pair + half, 1), :] = top + jnp.log(total)
             o = dot(v_t[half * HEAD_DIM : (half + 1) * HEAD_DIM, :], e.astype(BF))
             mixed_t.append(o * (1.0 / total))
         mixed_ref[:, cols] = jnp.concatenate(mixed_t, axis=0).T.astype(BF)
-        return carry
-
-    lax.fori_loop(0, HEADS // 2, one_pair, 0)
+        return worst
+
+    keys = k_ref.shape[0]
+    start = jnp.zeros((1, rows), F32)
+    worst = lax.fori_loop(
+        0, HEADS // 2, functools.partial(one_pair, keys // 4), start, unroll=True
+    )
+
+    @pl.when(jnp.max(worst) > LARGEST_SUM)
+    def _():
+        lax.fori_loop(0, HEADS // 2, functools.partial(one_pair, keys), start)
 
 
 def mlp_kernel(stepped, ids, present, x0, mixed, *refs):
@@ -627,43 +627,29 @@
     return [own, xor_pass(own, "section", 1), near, xor_pass(near, "section", 1)]
 
 
-def first_frames(ids, pair, weight):
+def first_frames(ids, present, pair, gouts, weight):
     rows = sds(pair.shape[1:], BF)
     half = sds((pair.shape[1] // 2, pair.shape[2]), BF)
-    block, part = call(outgoing_kernel, [rows, half], [ids, pair], "outgoing", 1_000_000)
+    block, part = call(
+        outgoing_kernel, [sds(pair.shape, BF), half], [ids, pair, gouts], "outgoing", 1_000_000
+    )
     mine = lax.ppermute(block, ("section", "shard"), split_pairs(1, 2))
     half_mine = xor_pass(part, "shard", 3)
     parts = shard_spread(weight)
     mine, half_mine = after([mine, half_mine], *parts[1:])
     other, half_other = (xor_pass(got, "section", 1) for got in (mine, half_mine))
-    frames = call(
+    *frames, gout = call(
         arrange_kernel,
-        [rows] * 4,
-        [ids, pair, mine, other, half_mine, half_other],
+        [rows] * 5,
+        [ids, present, pair, gouts, mine, other, half_mine, half_other],
         "arrange",
         1_000_000,
-    )
-    return block, list(frames), both_cores(parts)
-
-
-def to_clip(ids, present, pair):
-    count = lax.axis_size("shard")
-    pairs = [((i >> 1) * count + i, (i >> 1) * count + (i ^ 2)) for i in range(count)]
-    rows = sds(pair.shape[1:], BF)
-    (away,) = call(away_kernel, [rows], [ids, pair], "away", 1_000_000)
-    got = lax.ppermute(away, ("section", "shard"), pairs)
-    (home,) = call(
-        home_kernel,
-        [rows],
-        [ids, present, pair, got],
-        "home",
-        1_000_000,
         scalars=2,
     )
-    return home
-
-
-def from_clip(ids, pair):
+    return block, frames, gout, both_cores(parts)
+
+
+def from_clip(ids, pair, ties):
     count = lax.axis_size("shard")
 
     def pairs(flip):
@@ -676,7 +662,7 @@
 
     both = ("section", "shard")
     rows = sds(pair[0].shape, BF)
-    same, swap = call(order_kernel, [rows, rows], [ids, *pair], "order", 1_000_000)
+    same, swap = call(order_kernel, [rows, rows], [ids, *pair], "order", 1_000_000, ties=ties)
     return lax.ppermute(same, both, pairs(0)), lax.ppermute(swap, both, pairs(1))
 
 
@@ -783,10 +769,10 @@
     ids = jnp.stack([shard, section, place, replica]).astype(jnp.int32)
     own_rows = D // SHARDS
 
-    arrived, frames, qkv_part = first_frames(ids, inputs[0], qkv_weight[0])
-
-    (late,) = after([cotangent[0]], arrived)
-    gout_last = to_clip(ids, clip_present, late)
+    ready, frames, gout_last, qkv_part = first_frames(
+        ids, clip_present, inputs[0], cotangent[0], qkv_weight[0]
+    )
+
 
     half_rows = own_rows // 2
     packed = sds((half_rows, 9 * D), BF)
@@ -797,7 +783,7 @@
         "pack",
         1_000_000,
         raw=3,
-        ties=(arrived,),
+        ties=(ready,),
         scratch=[pltpu.SemaphoreType.DMA((12,))],
     )
     got = xor_pass(swap, "section", 1)
@@ -808,7 +794,7 @@
         "small",
         1_000_000,
         scalars=0,
-        ties=(arrived,),
+        ties=(ready,),
     )
     other_small = xor_pass(small, "section", 1)
     both = sds((16, D), F32)
@@ -817,7 +803,7 @@
     )
     rest_zero, rest_one = call(
         pick_kernel, [packed, packed], [ids, stay, got], "pick", 1_000_000,
-        ties=(*qkv_part[1:4], gout_last),
+        ties=(qkv_part[1],),
     )
     rest_part = shard_spread(rest_zero)
 
@@ -840,12 +826,14 @@
             [ids, *frames, *qkv_part, small],
             "attend",
             4_000_000_000,
+            ties=last_other if layer == 1 else (),
         )
         if layer == 0:
             last_parts = shard_steps(after([rest_one], mixed)[0])
             rest_part = both_cores([rest_part[0], *after(rest_part[1:], mixed)])
         else:
-            rest_part = both_cores([last_parts[0], *after(last_parts[1:], mixed)])
+            (pair,) = after(last_parts[2:], mixed)
+            rest_part = [*last_parts[:2], pair, *last_other, xor_pass(pair, "section", 1)]
         out, resid, z, slope, w_out, w_up, w_down = call(
             functools.partial(mlp_kernel, layer == 1),
             [
@@ -868,9 +856,9 @@
         outs.append(out)
         if layer == 0:
             frames = clip_frames(out)
+            last_other = tuple(xor_pass(part, "section", 1) for part in last_parts)
             last_parts = shard_steps_end(*last_parts, frames[2])
 
-    outs_back = from_clip(ids, outs)
     gout = gout_last
     shares = [None, None]
     grads = [None, None]
@@ -929,11 +917,12 @@
         )
         if layer == 1:
             keep, *send = parts
-            parts = [(keep, *after(send, back, *outs_back))]
+            parts = [(keep, *after(send, back))]
             ((own, first_out, second_out),) = section_sum(parts, True, ())
             before = (first_out,)
         else:
-            parts = section_sum((parts[:3], parts[3:]), False, (back, late))
+            outs_back = from_clip(ids, outs, (da_swap,))
+            parts = section_sum((parts[:3], parts[3:]), False, (back, late, *outs_back))
         (gin,) = call(
             norm_back_kernel,
             [sds((rows, D), BF)],
@@ -958,7 +947,7 @@
             ]
 
     outputs_local = clips_of(ids, *outs_back)
-    grads_local = clips_of(ids, *from_clip(ids, grads))
+    grads_local = clips_of(ids, *from_clip(ids, grads, ()))
     n = own_rows // replicas
     (away,) = call(
         functools.partial(choose_kernel, n),

time: 166 us -> 163 us (0.982)
  Pallas kernels: 55.9 us -> 50.1 us
  waiting for transfers between devices: 48.9 us -> 53 us
  starting transfers between devices: 55.8 us -> 52.6 us
  local copies, waits for them, and re-layouts: 3.58 us -> 5.42 us
    ppermute x51, waiting for transfers between devices: 39.3 us -> 46.4 us  [xor_pass(): return lax.ppermute(x, axis, pairs)]
    pallas_call x33 -> x31, Pallas kernels: 55.9 us -> 50.1 us  [call(): pl.pallas_call(body, out_shape=outs, in_specs=[smem] * scalars + [vmem] *...]
    ppermute x1 -> x0, starting transfers between devices: 2.42 us -> none  [to_clip(): got = lax.ppermute(away, ('section', 'shard'), pairs)]
    unnamed x27 -> x30, local copies, waits for them, and re-layouts: 3.58 us -> 5.42 us
    ppermute x1 -> x0, waiting for transfers between devices: 1.75 us -> none  [to_clip(): got = lax.ppermute(away, ('section', 'shard'), pairs)]
    ppermute x2, waiting for transfers between devices: 2.37 us -> 0.62 us  [from_clip(): lax.ppermute(swap, both, pairs(1))]
  transfers between devices with their start and end apart: 61 -> 60, of which waited for: 30 -> 28; matrix products, arithmetic and copies ran while one was open for 0% -> 0% of each run, Pallas kernels for 26% -> 23%
where the time goes in v1:
time: 163 us; the launch traced here: 162 us
  waiting for transfers between devices  53 us (33%)
  starting transfers between devices  52.6 us (32%)
  Pallas kernels  50.1 us (31%)
  local copies, waits for them, and re-layouts  5.42 us (3%)
    pallas_call x31, Pallas kernels, call(): pl.pallas_call(body, out_shape=outs, in_specs=[smem] * scalars + [vmem] *...  50.1 us
    ppermute x51, waiting for transfers between devices, xor_pass(): return lax.ppermute(x, axis, pairs)  46.4 us
    ppermute x51, starting transfers between devices, xor_pass(): return lax.ppermute(x, axis, pairs)  39.4 us
    unnamed x30, local copies, waits for them, and re-layouts  5.42 us
    ppermute x2, starting transfers between devices, from_clip(): lax.ppermute(swap, both, pairs(1))  4.69 us
  transfers between devices with their start and end apart: 60, of which 28 were waited for; matrix products, arithmetic and copies ran while one was open for 0% of the time, Pallas kernels for 23%

profile of v1, /device:TPU:0, one launch (start us, length us, event | category | flops | bytes accessed | tf_op | source)
XLA Modules:
  0.0 162.4 jit_solution(16380509364323545625)
XLA Ops:
  3.4 3.0 %collective-permute-start = (bf16[2,256,384]{2,1,0:T(8,128)(2,1)S(1)}, bf16[2,256,384]{2,1,0:T(8,128)(2,1)S(1)}, u32[]{:S(2)}, u32[]{:S(2)}) collective-permute-start(bf16[2,256,384]{2,1,0:T(8,128)(2,1)S(1)} %get-tuple-element.126.refs_3_.refs_4_), channel_id=1, source_target_pairs={{0,1},{1,0},{2,3},{3,2},{16,18},{17,19},{18,16},{19,17},{4,5},{5,4... | collective-permute-start | bytes 1179656 | tf_op jit(solution)/shard_map/ppermute | solution.py:636
  7.9 1.9 %collective-permute-start.2 = (bf16[96,1152]{1,0:T(8,128)(2,1)}, bf16[96,1152]{1,0:T(8,128)(2,1)S(1)}, u32[]{:S(2)}, u32[]{:S(2)}) collective-permute-start(bf16[96,1152]{1,0:T(8,128)(2,1)} %bitcast.30), channel_id=1, source_target_pairs={{0,1},{1,0},{2,3},{3,2},{4,5},{5,4},{6,7},{7,6},{8,9},{9,8},{10,11... | collective-permute-start | bytes 663560 | tf_op jit(solution)/shard_map/ppermute | solution.py:33
  15.0 10.2 %collective-permute-done.1.refs_1_ = bf16[128,384]{1,0:T(8,128)(2,1)S(1)} collective-permute-done((bf16[128,384]{1,0:T(8,128)(2,1)S(1)}, bf16[128,384]{1,0:T(8,128)(2,1)S(1)}, u32[]{:S(2)}, u32[]{:S(2)}) %collective-permute-start.1) | collective-permute-done | bytes 98336 | tf_op jit(solution)/shard_map/ppermute | solution.py:33
  27.4 1.5 collective-permute-start.15
  29.0 1.5 collective-permute-start.14
  34.4 5.0 %attend.2 = (bf16[384,1152]{1,0:T(8,128)(2,1)S(1)}, bf16[1024,384]{1,0:T(8,128)(2,1)S(1)}, bf16[256,384]{1,0:T(8,128)(2,1)S(1)}, bf16[1024,384]{1,0:T(8,128)(2,1...) custom-call(s32[4]{0:T(128)S(1)} %pad_add_fusion.refs_0_, ...), custom_call_target="tpu_custom_call" | custom-call | flops 4000000 | bytes 6225 | tf_op jit(solution)/shard_map/attend/pallas_call | solution.py:47
  39.4 5.9 %collective-permute-done.14.refs_1_ = bf16[48,3456]{1,0:T(8,128)(2,1)S(1)} collective-permute-done((bf16[48,3456]{1,0:T(8,128)(2,1)S(1)}, bf16[48,3456]{1,0:T(8,128)(2,1)S(1)}, u32[]{:S(2)}, u32[]{:S(2)}) %collective-permute-start.14) | collective-permute-done | bytes 331808 | tf_op jit(solution)/shard_map/ppermute | solution.py:33
  47.9 2.5 %mlp.2 = (bf16[256,384]{1,0:T(8,128)(2,1)S(1)}, f32[256,384]{1,0:T(8,128)S(1)}, bf16[256,1536]{1,0:T(8,128)(2,1)S(1)}, bf16[256,1536]{1,0:T(8,128)(2,1)S(1)}, bf...) custom-call(s32[4]{0:T(128)S(1)} %pad_add_fusion.refs_0_, ...), custom_call_target="tpu_custom_call" | custom-call | flops 2000000 | bytes 7888 | tf_op jit(solution)/shard_map/mlp/pallas_call | solution.py:47
  53.0 4.4 %collective-permute-done.21.refs_3_.refs_2_ = bf16[256,384]{1,0:T(8,128)(2,1)S(1)} collective-permute-done((bf16[256,384]{1,0:T(8,128)(2,1)S(1)}, bf16[256,384]{1,0:T(8,128)(2,1)S(1)}, u32[]{:S(2)}, u32[]{:S(2)}) %collective-permute-start.21) | collective-permute-done | bytes 196640 | tf_op jit(solution)/shard_map/ppermute | solution.py:33
  60.8 5.1 %attend.3 = (bf16[384,1152]{1,0:T(8,128)(2,1)S(1)}, bf16[1024,384]{1,0:T(8,128)(2,1)S(1)}, bf16[256,384]{1,0:T(8,128)(2,1)S(1)}, bf16[1024,384]{1,0:T(8,128)(2,1...) custom-call(s32[4]{0:T(128)S(1)} %pad_add_fusion.refs_0_, ...), custom_call_target="tpu_custom_call" | custom-call | flops 4000000 | bytes 6225 | tf_op jit(solution)/shard_map/attend/pallas_call | solution.py:47
  65.9 2.3 %collective-permute-done.26.refs_0_ = bf16[2,48,3456]{2,1,0:T(8,128)(2,1)S(1)} collective-permute-done((bf16[2,48,3456]{2,1,0:T(8,128)(2,1)S(1)}, bf16[2,48,3456]{2,1,0:T(8,128)(2,1)S(1)}, u32[]{:S(2)}, u32[]{:S(2)}) %collective-permute-start.26) | collective-permute-done | bytes 663584 | tf_op jit(solution)/shard_map/ppermute | solution.py:618
  68.2 2.1 %collective-permute-done.27.refs_9_ = bf16[2,48,3456]{2,1,0:T(8,128)(2,1)S(1)} collective-permute-done((bf16[2,48,3456]{2,1,0:T(8,128)(2,1)S(1)}, bf16[2,48,3456]{2,1,0:T(8,128)(2,1)S(1)}, u32[]{:S(2)}, u32[]{:S(2)}) %collective-permute-start.27) | collective-permute-done | bytes 663584 | tf_op jit(solution)/shard_map/ppermute | solution.py:33
  70.3 2.5 %mlp.3 = (bf16[256,384]{1,0:T(8,128)(2,1)S(1)}, f32[256,384]{1,0:T(8,128)S(1)}, bf16[256,1536]{1,0:T(8,128)(2,1)S(1)}, bf16[256,1536]{1,0:T(8,128)(2,1)S(1)}, bf...) custom-call(s32[4]{0:T(128)S(1)} %pad_add_fusion.refs_0_, ...), custom_call_target="tpu_custom_call" | custom-call | flops 2000000 | bytes 7888 | tf_op jit(solution)/shard_map/mlp/pallas_call | solution.py:47
  74.3 6.0 %attend_back.2 = (f32[256,384]{1,0:T(8,128)S(1)}, f32[256,384]{1,0:T(8,128)S(1)}, bf16[2,256,384]{2,1,0:T(8,128)(2,1)S(1)}, bf16[256,384]{1,0:T(8,128)(2,1)S(1)}...) custom-call(bf16[256,384]{1,0:T(8,128)(2,1)S(1)} %get-tuple-element.151.refs_0_, ...), custom_call_target="tpu_custom_call" | custom-call | flops 8000000 | bytes 6803 | tf_op jit(solution)/shard_map/attend_back/pallas_call | solution.py:47
  80.5 1.6 collective-permute-done.28.refs_1_
  83.4 3.7 %grad.2 = (bf16[4,304,768]{2,1,0:T(8,128)(2,1)S(1)}, bf16[2,304,768]{2,1,0:T(8,128)(2,1)S(1)}, bf16[2,304,768]{2,1,0:T(8,128)(2,1)S(1)}) custom-call(s32[4]{0:T(128)S(1)} %pad_add_fusion.refs_0_, bf16[256,384]{1,0:T(8,128)(2,1)S(1)} %get-tuple-element.178.refs_1_, bf16[256,1536]{1,0:T(8,128)(2,1)S(1)} %get-tuple-element.179.refs_2_, ...), custom_call_target="tpu_custom_call" | custom-call | flops 4000000 | bytes 8706 | tf_op jit(solution)/shard_map/grad/pallas_call | solution.py:47
  87.0 2.1 %collective-permute-done.29.refs_2_ = bf16[256,384]{1,0:T(8,128)(2,1)S(1)} collective-permute-done((bf16[256,384]{1,0:T(8,128)(2,1)S(1)}, bf16[256,384]{1,0:T(8,128)(2,1)S(1)}, u32[]{:S(2)}, u32[]{:S(2)}) %collective-permute-start.29) | collective-permute-done | bytes 196640 | tf_op jit(solution)/shard_map/ppermute | solution.py:33
  89.6 2.0 %collective-permute-done.30.refs_1_ = bf16[2,304,768]{2,1,0:T(8,128)(2,1)S(1)} collective-permute-done((bf16[2,304,768]{2,1,0:T(8,128)(2,1)S(1)}, bf16[2,304,768]{2,1,0:T(8,128)(2,1)S(1)}, u32[]{:S(2)}, u32[]{:S(2)}) %collective-permute-start.30) | collective-permute-done | bytes 933920 | tf_op jit(solution)/shard_map/ppermute | solution.py:33
  96.5 5.9 %attend_back.3 = (f32[256,384]{1,0:T(8,128)S(1)}, f32[256,384]{1,0:T(8,128)S(1)}, bf16[2,256,384]{2,1,0:T(8,128)(2,1)S(1)}, bf16[256,384]{1,0:T(8,128)(2,1)S(1)}...) custom-call(bf16[256,384]{1,0:T(8,128)(2,1)S(1)} %get-tuple-element.147.refs_0_, ...), custom_call_target="tpu_custom_call" | custom-call | flops 8000000 | bytes 6803 | tf_op jit(solution)/shard_map/attend_back/pallas_call | solution.py:47
  103.8 2.3 %collective-permute-start.33 = (bf16[256,384]{1,0:T(8,128)(2,1)S(1)}, bf16[256,384]{1,0:T(8,128)(2,1)S(1)}, u32[]{:S(2)}, u32[]{:S(2)}) collective-permute-start(bf16[256,384]{1,0:T(8,128)(2,1)S(1)} %get-tuple-element.194), channel_id=1, source_target_pairs={{0,16},{1,17},{2,0},{3,1},{16,18},{17,19},{18,2},{19,3},{4,20},{5,... | collective-permute-start | bytes 589832 | tf_op jit(solution)/shard_map/ppermute | solution.py:666
  107.1 3.4 %grad.3 = (bf16[4,192,768]{2,1,0:T(8,128)(2,1)S(1)}, bf16[2,192,768]{2,1,0:T(8,128)(2,1)S(1)}, bf16[2,192,768]{2,1,0:T(8,128)(2,1)S(1)}, bf16[4,112,768]{2,1,0:T...) custom-call(s32[4]{0:T(128)S(1)} %pad_add_fusion.refs_0_, ...), custom_call_target="tpu_custom_call" | custom-call | flops 4000000 | bytes 8706 | tf_op jit(solution)/shard_map/grad/pallas_call | solution.py:47
  115.2 2.4 %collective-permute-start.37 = (bf16[256,384]{1,0:T(8,128)(2,1)S(1)}, bf16[256,384]{1,0:T(8,128)(2,1)S(1)}, u32[]{:S(2)}, u32[]{:S(2)}) collective-permute-start(bf16[256,384]{1,0:T(8,128)(2,1)S(1)} %get-tuple-element.199), channel_id=1, source_target_pairs={{0,16},{1,17},{2,0},{3,1},{16,18},{17,19},{18,2},{19,3},{4,20},{5,... | collective-permute-start | bytes 589832 | tf_op jit(solution)/shard_map/ppermute | solution.py:666
  117.6 2.2 %collective-permute-done.43.refs_7_.refs_3_ = bf16[304,768]{1,0:T(8,128)(2,1)S(1)} collective-permute-done((bf16[304,768]{1,0:T(8,128)(2,1)S(1)}, bf16[304,768]{1,0:T(8,128)(2,1)S(1)}, u32[]{:S(2)}, u32[]{:S(2)}) %collective-permute-start.43) | collective-permute-done | bytes 466976 | tf_op jit(solution)/shard_map/ppermute | solution.py:718
  123.2 1.6 %collective-permute-start.47 = (bf16[88,768]{1,0:T(8,128)(2,1)S(1)}, bf16[88,768]{1,0:T(8,128)(2,1)S(1)}, u32[]{:S(2)}, u32[]{:S(2)}) collective-permute-start(bf16[88,768]{1,0:T(8,128)(2,1)S(1)} %get-tuple-element.221), channel_id=1, source_target_pairs={{0,4},{4,0},{8,12},{12,8},{1,5},{5,1},{9,13},{13,9},{2,6},{6,2},{1... | collective-permute-start | bytes 405512 | tf_op jit(solution)/shard_map/ppermute | solution.py:33
  128.3 2.6 %collective-permute-start.48 = (bf16[88,768]{1,0:T(8,128)(2,1)S(1)}, bf16[88,768]{1,0:T(8,128)(2,1)S(1)}, u32[]{:S(2)}, u32[]{:S(2)}) collective-permute-start(bf16[88,768]{1,0:T(8,128)(2,1)S(1)} %get-tuple-element.222), channel_id=1, source_target_pairs={{0,8},{4,12},{8,0},{12,4},{1,9},{5,13},{9,1},{13,5},{2,10},{6,14},... | collective-permute-start | bytes 405512 | tf_op jit(solution)/shard_map/ppermute | solution.py:33
  133.6 2.8 %collective-permute-done.55.refs_4_ = bf16[112,768]{1,0:T(8,128)(2,1)S(1)} collective-permute-done((bf16[112,768]{1,0:T(8,128)(2,1)S(1)}, bf16[112,768]{1,0:T(8,128)(2,1)S(1)}, u32[]{:S(2)}, u32[]{:S(2)}) %collective-permute-start.55) | collective-permute-done | bytes 172064 | tf_op jit(solution)/shard_map/ppermute | solution.py:33
  141.3 1.7 %collective-permute-start.56 = (bf16[40,768]{1,0:T(8,128)(2,1)S(1)}, bf16[40,768]{1,0:T(8,128)(2,1)S(1)}, u32[]{:S(2)}, u32[]{:S(2)}) collective-permute-start(bf16[40,768]{1,0:T(8,128)(2,1)S(1)} %get-tuple-element.233), channel_id=1, source_target_pairs={{0,4},{4,0},{8,12},{12,8},{1,5},{5,1},{9,13},{13,9},{2,6},{6,2},{1... | collective-permute-start | bytes 184328 | tf_op jit(solution)/shard_map/ppermute | solution.py:33
  142.9 2.6 %collective-permute-start.57 = (bf16[40,768]{1,0:T(8,128)(2,1)S(1)}, bf16[40,768]{1,0:T(8,128)(2,1)S(1)}, u32[]{:S(2)}, u32[]{:S(2)}) collective-permute-start(bf16[40,768]{1,0:T(8,128)(2,1)S(1)} %get-tuple-element.234), channel_id=1, source_target_pairs={{0,8},{4,12},{8,0},{12,4},{1,9},{5,13},{9,1},{13,5},{2,10},{6,14},... | collective-permute-start | bytes 184328 | tf_op jit(solution)/shard_map/ppermute | solution.py:33
  145.8 1.9 %collective-permute-done.45.refs_3_ = bf16[192,768]{1,0:T(8,128)(2,1)S(1)} collective-permute-done((bf16[192,768]{1,0:T(8,128)(2,1)S(1)}, bf16[192,768]{1,0:T(8,128)(2,1)S(1)}, u32[]{:S(2)}, u32[]{:S(2)}) %collective-permute-start.45) | collective-permute-done | bytes 294944 | tf_op jit(solution)/shard_map/ppermute | solution.py:33
  149.7 2.5 %collective-permute-start.51 = (bf16[48,768]{1,0:T(8,128)(2,1)S(1)}, bf16[48,768]{1,0:T(8,128)(2,1)S(1)}, u32[]{:S(2)}, u32[]{:S(2)}) collective-permute-start(bf16[48,768]{1,0:T(8,128)(2,1)S(1)} %get-tuple-element.226), channel_id=1, source_target_pairs={{0,8},{4,12},{8,0},{12,4},{1,9},{5,13},{9,1},{13,5},{2,10},{6,14},... | collective-permute-start | bytes 221192 | tf_op jit(solution)/shard_map/ppermute | solution.py:33
  153.2 3.2 %collective-permute-done.51 = bf16[48,768]{1,0:T(8,128)(2,1)S(1)} collective-permute-done((bf16[48,768]{1,0:T(8,128)(2,1)S(1)}, bf16[48,768]{1,0:T(8,128)(2,1)S(1)}, u32[]{:S(2)}, u32[]{:S(2)}) %collective-permute-start.51) | collective-permute-done | bytes 73760 | tf_op jit(solution)/shard_map/ppermute | solution.py:33
  156.5 1.9 %collective-permute-done.52 = bf16[48,768]{1,0:T(8,128)(2,1)S(1)} collective-permute-done((bf16[48,768]{1,0:T(8,128)(2,1)S(1)}, bf16[48,768]{1,0:T(8,128)(2,1)S(1)}, u32[]{:S(2)}, u32[]{:S(2)}) %collective-permute-start.52) | collective-permute-done | bytes 73760 | tf_op jit(solution)/shard_map/ppermute | solution.py:33
  (160 shorter events, 61.0 us)
Async XLA Ops:
  3.4 21.9 %collective-permute-start = (bf16[2,256,384]{2,1,0:T(8,128)(2,1)S(1)}, bf16[2,256,384]{2,1,0:T(8,128)(2,1)S(1)}, u32[]{:S(2)}, u32[]{:S(2)}) collective-permute-start(bf16[2,256,384]{2,1,0:T(8,128)(2,1)S(1)} %get-tuple-element.126.refs_3_.refs_4_), channel_id=1, source_target_pairs={{0,1},{1,0},{2,3},{3,2},{16,18},{17,19},{18,16},{19,17},{4,5},{5,4... | collective-permute-start | bytes 1179656 | tf_op jit(solution)/shard_map/ppermute | solution.py:636
  6.4 18.8 %collective-permute-start.4 = (bf16[96,1152]{1,0:T(8,128)(2,1)}, bf16[96,1152]{1,0:T(8,128)(2,1)S(1)}, u32[]{:S(2)}, u32[]{:S(2)}) collective-permute-start(bf16[96,1152]{1,0:T(8,128)(2,1)} %bitcast.28), channel_id=1, source_target_pairs={{0,3},{1,2},{2,1},{3,0},{4,7},{5,6},{6,5},{7,4},{8,11},{9,10},{10,... | collective-permute-start | bytes 663560 | tf_op jit(solution)/shard_map/ppermute | solution.py:33
  7.9 17.4 %collective-permute-start.3 = (bf16[96,1152]{1,0:T(8,128)(2,1)}, bf16[96,1152]{1,0:T(8,128)(2,1)S(1)}, u32[]{:S(2)}, u32[]{:S(2)}) collective-permute-start(bf16[96,1152]{1,0:T(8,128)(2,1)} %bitcast.29), channel_id=1, source_target_pairs={{0,2},{1,3},{2,0},{3,1},{4,6},{5,7},{6,4},{7,5},{8,10},{9,11},{10,... | collective-permute-start | bytes 663560 | tf_op jit(solution)/shard_map/ppermute | solution.py:33
  7.9 17.3 %collective-permute-start.2 = (bf16[96,1152]{1,0:T(8,128)(2,1)}, bf16[96,1152]{1,0:T(8,128)(2,1)S(1)}, u32[]{:S(2)}, u32[]{:S(2)}) collective-permute-start(bf16[96,1152]{1,0:T(8,128)(2,1)} %bitcast.30), channel_id=1, source_target_pairs={{0,1},{1,0},{2,3},{3,2},{4,5},{5,4},{6,7},{7,6},{8,9},{9,8},{10,11... | collective-permute-start | bytes 663560 | tf_op jit(solution)/shard_map/ppermute | solution.py:33
  9.9 15.3 %collective-permute-start.1 = (bf16[128,384]{1,0:T(8,128)(2,1)S(1)}, bf16[128,384]{1,0:T(8,128)(2,1)S(1)}, u32[]{:S(2)}, u32[]{:S(2)}) collective-permute-start(bf16[128,384]{1,0:T(8,128)(2,1)S(1)} %get-tuple-element.127), channel_id=1, source_target_pairs={{0,3},{1,2},{2,1},{3,0},{4,7},{5,6},{6,5},{7,4},{8,11},{9,10},{10,... | collective-permute-start | bytes 294920 | tf_op jit(solution)/shard_map/ppermute | solution.py:33
  25.3 7.2 %collective-permute-start.5 = (bf16[2,256,384]{2,1,0:T(8,128)(2,1)S(1)}, bf16[2,256,384]{2,1,0:T(8,128)(2,1)S(1)}, u32[]{:S(2)}, u32[]{:S(2)}) collective-permute-start(bf16[2,256,384]{2,1,0:T(8,128)(2,1)S(1)} %get-tuple-element.128.refs_4_), channel_id=1, source_target_pairs={{0,16},{16,0},{1,17},{17,1},{2,18},{18,2},{3,19},{19,3},{4,20},{20... | collective-permute-start | bytes 1179656 | tf_op jit(solution)/shard_map/ppermute | solution.py:33
  27.4 12.0 %collective-permute-start.15 = (bf16[48,3456]{1,0:T(8,128)(2,1)S(1)}, bf16[48,3456]{1,0:T(8,128)(2,1)S(1)}, u32[]{:S(2)}, u32[]{:S(2)}) collective-permute-start(bf16[48,3456]{1,0:T(8,128)(2,1)S(1)} %get-tuple-element.138.refs_4_), channel_id=1, source_target_pairs={{0,3},{1,2},{2,1},{3,0},{4,7},{5,6},{6,5},{7,4},{8,11},{9,10},{10,... | collective-permute-start | bytes 995336 | tf_op jit(solution)/shard_map/ppermute | solution.py:33
  29.0 16.4 %collective-permute-start.14 = (bf16[48,3456]{1,0:T(8,128)(2,1)S(1)}, bf16[48,3456]{1,0:T(8,128)(2,1)S(1)}, u32[]{:S(2)}, u32[]{:S(2)}) collective-permute-start(bf16[48,3456]{1,0:T(8,128)(2,1)S(1)} %get-tuple-element.138.refs_4_), channel_id=1, source_target_pairs={{0,2},{1,3},{2,0},{3,1},{4,6},{5,7},{6,4},{7,5},{8,10},{9,11},{10,... | collective-permute-start | bytes 995336 | tf_op jit(solution)/shard_map/ppermute | solution.py:33
  30.5 14.8 %collective-permute-start.13 = (bf16[48,3456]{1,0:T(8,128)(2,1)S(1)}, bf16[48,3456]{1,0:T(8,128)(2,1)S(1)}, u32[]{:S(2)}, u32[]{:S(2)}) collective-permute-start(bf16[48,3456]{1,0:T(8,128)(2,1)S(1)} %get-tuple-element.138.refs_4_), channel_id=1, source_target_pairs={{0,1},{1,0},{2,3},{3,2},{4,5},{5,4},{6,7},{7,6},{8,9},{9,8},{10,11... | collective-permute-start | bytes 995336 | tf_op jit(solution)/shard_map/ppermute | solution.py:33
  34.2 12.9 %collective-permute-start.16 = (bf16[48,3456]{1,0:T(8,128)(2,1)S(1)}, bf16[48,3456]{1,0:T(8,128)(2,1)S(1)}, u32[]{:S(2)}, u32[]{:S(2)}) collective-permute-start(bf16[48,3456]{1,0:T(8,128)(2,1)S(1)} %get-tuple-element.138.refs_4_), channel_id=1, source_target_pairs={{0,16},{16,0},{1,17},{17,1},{2,18},{18,2},{3,19},{19,3},{4,20},{20... | collective-permute-start | bytes 995336 | tf_op jit(solution)/shard_map/ppermute | solution.py:33
  45.9 7.1 %collective-permute-start.24 = (bf16[48,3456]{1,0:T(8,128)(2,1)S(1)}, bf16[48,3456]{1,0:T(8,128)(2,1)S(1)}, u32[]{:S(2)}, u32[]{:S(2)}) collective-permute-start(bf16[48,3456]{1,0:T(8,128)(2,1)S(1)} %after.7.refs_0_.refs_4_), channel_id=1, source_target_pairs={{0,1},{1,0},{2,3},{3,2},{16,18},{17,19},{18,16},{19,17},{4,5},{5,4... | collective-permute-start | bytes 995336 | tf_op jit(solution)/shard_map/ppermute | solution.py:605
  50.4 7.0 %collective-permute-start.21 = (bf16[256,384]{1,0:T(8,128)(2,1)S(1)}, bf16[256,384]{1,0:T(8,128)(2,1)S(1)}, u32[]{:S(2)}, u32[]{:S(2)}) collective-permute-start(bf16[256,384]{1,0:T(8,128)(2,1)S(1)} %get-tuple-element.142.refs_1_.refs_2_.refs_3_), channel_id=1, source_target_pairs={{0,1},{1,0},{2,3},{3,2},{4,5},{5,4},{6,7},{7,6},{8,9},{9,8},{10,11... | collective-permute-start | bytes 589832 | tf_op jit(solution)/shard_map/ppermute | solution.py:33
  57.5 10.7 %collective-permute-start.26 = (bf16[2,48,3456]{2,1,0:T(8,128)(2,1)S(1)}, bf16[2,48,3456]{2,1,0:T(8,128)(2,1)S(1)}, u32[]{:S(2)}, u32[]{:S(2)}) collective-permute-start(bf16[2,48,3456]{2,1,0:T(8,128)(2,1)S(1)} %stack.21), channel_id=1, source_target_pairs={{0,2},{1,3},{2,0},{3,1},{16,17},{17,16},{18,19},{19,18},{4,6},{5,7... | collective-permute-start | bytes 1990664 | tf_op jit(solution)/shard_map/ppermute | solution.py:618
  82.1 7.0 %collective-permute-start.29 = (bf16[256,384]{1,0:T(8,128)(2,1)S(1)}, bf16[256,384]{1,0:T(8,128)(2,1)S(1)}, u32[]{:S(2)}, u32[]{:S(2)}) collective-permute-start(bf16[256,384]{1,0:T(8,128)(2,1)S(1)} %fusion.1.refs_14_), channel_id=1, source_target_pairs={{0,1},{1,0},{2,3},{3,2},{4,5},{5,4},{6,7},{7,6},{8,9},{9,8},{10,11... | collective-permute-start | bytes 589832 | tf_op jit(solution)/shard_map/ppermute | solution.py:33
  93.4 17.2 %collective-permute-start.42 = (bf16[2,304,768]{2,1,0:T(8,128)(2,1)S(1)}, bf16[2,304,768]{2,1,0:T(8,128)(2,1)S(1)}, u32[]{:S(2)}, u32[]{:S(2)}) collective-permute-start(bf16[2,304,768]{2,1,0:T(8,128)(2,1)S(1)} %get-tuple-element.191.refs_8_), channel_id=1, source_target_pairs={{0,1},{1,0},{2,3},{3,2},{16,18},{17,19},{18,16},{19,17},{4,5},{5,4... | collective-permute-start | bytes 2801672 | tf_op jit(solution)/shard_map/ppermute | solution.py:705
  103.1 8.1 %collective-permute-start.32 = (bf16[256,384]{1,0:T(8,128)(2,1)S(1)}, bf16[256,384]{1,0:T(8,128)(2,1)S(1)}, u32[]{:S(2)}, u32[]{:S(2)}) collective-permute-start(bf16[256,384]{1,0:T(8,128)(2,1)S(1)} %get-tuple-element.193), channel_id=1, source_target_pairs={{0,0},{1,1},{2,16},{3,17},{16,2},{17,3},{18,18},{19,19},{4,4},{5,5... | collective-permute-start | bytes 589832 | tf_op jit(solution)/shard_map/ppermute | solution.py:666
  103.8 9.1 %collective-permute-start.33 = (bf16[256,384]{1,0:T(8,128)(2,1)S(1)}, bf16[256,384]{1,0:T(8,128)(2,1)S(1)}, u32[]{:S(2)}, u32[]{:S(2)}) collective-permute-start(bf16[256,384]{1,0:T(8,128)(2,1)S(1)} %get-tuple-element.194), channel_id=1, source_target_pairs={{0,16},{1,17},{2,0},{3,1},{16,18},{17,19},{18,2},{19,3},{4,20},{5,... | collective-permute-start | bytes 589832 | tf_op jit(solution)/shard_map/ppermute | solution.py:666
  110.5 7.1 %collective-permute-start.38 = (bf16[2,192,768]{2,1,0:T(8,128)(2,1)S(1)}, bf16[2,192,768]{2,1,0:T(8,128)(2,1)S(1)}, u32[]{:S(2)}, u32[]{:S(2)}) collective-permute-start(bf16[2,192,768]{2,1,0:T(8,128)(2,1)S(1)} %get-tuple-element.209), channel_id=1, source_target_pairs={{0,16},{16,0},{1,17},{17,1},{2,18},{18,2},{3,19},{19,3},{4,20},{20... | collective-permute-start | bytes 1769480 | tf_op jit(solution)/shard_map/ppermute | solution.py:33
  111.2 8.6 %collective-permute-start.43 = (bf16[304,768]{1,0:T(8,128)(2,1)S(1)}, bf16[304,768]{1,0:T(8,128)(2,1)S(1)}, u32[]{:S(2)}, u32[]{:S(2)}) collective-permute-start(bf16[304,768]{1,0:T(8,128)(2,1)S(1)} %second.1), channel_id=1, source_target_pairs={{0,2},{1,3},{2,0},{3,1},{16,17},{17,16},{18,19},{19,18},{4,6},{5,7... | collective-permute-start | bytes 1400840 | tf_op jit(solution)/shard_map/ppermute | solution.py:718
  114.5 10.4 %collective-permute-start.36 = (bf16[256,384]{1,0:T(8,128)(2,1)S(1)}, bf16[256,384]{1,0:T(8,128)(2,1)S(1)}, u32[]{:S(2)}, u32[]{:S(2)}) collective-permute-start(bf16[256,384]{1,0:T(8,128)(2,1)S(1)} %get-tuple-element.198), channel_id=1, source_target_pairs={{0,0},{1,1},{2,16},{3,17},{16,2},{17,3},{18,18},{19,19},{4,4},{5,5... | collective-permute-start | bytes 589832 | tf_op jit(solution)/shard_map/ppermute | solution.py:666
  115.2 11.1 %collective-permute-start.37 = (bf16[256,384]{1,0:T(8,128)(2,1)S(1)}, bf16[256,384]{1,0:T(8,128)(2,1)S(1)}, u32[]{:S(2)}, u32[]{:S(2)}) collective-permute-start(bf16[256,384]{1,0:T(8,128)(2,1)S(1)} %get-tuple-element.199), channel_id=1, source_target_pairs={{0,16},{1,17},{2,0},{3,1},{16,18},{17,19},{18,2},{19,3},{4,20},{5,... | collective-permute-start | bytes 589832 | tf_op jit(solution)/shard_map/ppermute | solution.py:666
  120.2 10.7 %collective-permute-start.53 = (bf16[112,768]{1,0:T(8,128)(2,1)S(1)}, bf16[112,768]{1,0:T(8,128)(2,1)S(1)}, u32[]{:S(2)}, u32[]{:S(2)}) collective-permute-start(bf16[112,768]{1,0:T(8,128)(2,1)S(1)} %get-tuple-element.229), channel_id=1, source_target_pairs={{0,1},{1,0},{2,3},{3,2},{4,5},{5,4},{6,7},{7,6},{8,9},{9,8},{10,11... | collective-permute-start | bytes 516104 | tf_op jit(solution)/shard_map/ppermute | solution.py:33
  121.4 24.1 %collective-permute-start.44 = (bf16[192,768]{1,0:T(8,128)(2,1)S(1)}, bf16[192,768]{1,0:T(8,128)(2,1)S(1)}, u32[]{:S(2)}, u32[]{:S(2)}) collective-permute-start(bf16[192,768]{1,0:T(8,128)(2,1)S(1)} %get-tuple-element.216), channel_id=1, source_target_pairs={{0,1},{1,0},{2,3},{3,2},{4,5},{5,4},{6,7},{7,6},{8,9},{9,8},{10,11... | collective-permute-start | bytes 884744 | tf_op jit(solution)/shard_map/ppermute | solution.py:33
  124.9 7.4 %collective-permute-start.54 = (bf16[112,768]{1,0:T(8,128)(2,1)S(1)}, bf16[112,768]{1,0:T(8,128)(2,1)S(1)}, u32[]{:S(2)}, u32[]{:S(2)}) collective-permute-start(bf16[112,768]{1,0:T(8,128)(2,1)S(1)} %get-tuple-element.230), channel_id=1, source_target_pairs={{0,2},{1,3},{2,0},{3,1},{4,6},{5,7},{6,4},{7,5},{8,10},{9,11},{10,... | collective-permute-start | bytes 516104 | tf_op jit(solution)/shard_map/ppermute | solution.py:33
  126.3 10.2 %collective-permute-start.55 = (bf16[112,768]{1,0:T(8,128)(2,1)S(1)}, bf16[112,768]{1,0:T(8,128)(2,1)S(1)}, u32[]{:S(2)}, u32[]{:S(2)}) collective-permute-start(bf16[112,768]{1,0:T(8,128)(2,1)S(1)} %get-tuple-element.231), channel_id=1, source_target_pairs={{0,3},{1,2},{2,1},{3,0},{4,7},{5,6},{6,5},{7,4},{8,11},{9,10},{10,... | collective-permute-start | bytes 516104 | tf_op jit(solution)/shard_map/ppermute | solution.py:33
  128.3 13.0 %collective-permute-start.48 = (bf16[88,768]{1,0:T(8,128)(2,1)S(1)}, bf16[88,768]{1,0:T(8,128)(2,1)S(1)}, u32[]{:S(2)}, u32[]{:S(2)}) collective-permute-start(bf16[88,768]{1,0:T(8,128)(2,1)S(1)} %get-tuple-element.222), channel_id=1, source_target_pairs={{0,8},{4,12},{8,0},{12,4},{1,9},{5,13},{9,1},{13,5},{2,10},{6,14},... | collective-permute-start | bytes 405512 | tf_op jit(solution)/shard_map/ppermute | solution.py:33
  130.9 12.1 %collective-permute-start.49 = (bf16[88,768]{1,0:T(8,128)(2,1)S(1)}, bf16[88,768]{1,0:T(8,128)(2,1)S(1)}, u32[]{:S(2)}, u32[]{:S(2)}) collective-permute-start(bf16[88,768]{1,0:T(8,128)(2,1)S(1)} %get-tuple-element.223), channel_id=1, source_target_pairs={{0,12},{4,8},{8,4},{12,0},{1,13},{5,9},{9,5},{13,1},{2,14},{6,10},... | collective-permute-start | bytes 405512 | tf_op jit(solution)/shard_map/ppermute | solution.py:33
  132.2 15.5 %collective-permute-start.45 = (bf16[192,768]{1,0:T(8,128)(2,1)S(1)}, bf16[192,768]{1,0:T(8,128)(2,1)S(1)}, u32[]{:S(2)}, u32[]{:S(2)}) collective-permute-start(bf16[192,768]{1,0:T(8,128)(2,1)S(1)} %get-tuple-element.217), channel_id=1, source_target_pairs={{0,2},{1,3},{2,0},{3,1},{4,6},{5,7},{6,4},{7,5},{8,10},{9,11},{10,... | collective-permute-start | bytes 884744 | tf_op jit(solution)/shard_map/ppermute | solution.py:33
  136.5 11.2 %collective-permute-start.46 = (bf16[192,768]{1,0:T(8,128)(2,1)S(1)}, bf16[192,768]{1,0:T(8,128)(2,1)S(1)}, u32[]{:S(2)}, u32[]{:S(2)}) collective-permute-start(bf16[192,768]{1,0:T(8,128)(2,1)S(1)} %get-tuple-element.218), channel_id=1, source_target_pairs={{0,3},{1,2},{2,1},{3,0},{4,7},{5,6},{6,5},{7,4},{8,11},{9,10},{10,... | collective-permute-start | bytes 884744 | tf_op jit(solution)/shard_map/ppermute | solution.py:33
  141.3 10.9 %collective-permute-start.56 = (bf16[40,768]{1,0:T(8,128)(2,1)S(1)}, bf16[40,768]{1,0:T(8,128)(2,1)S(1)}, u32[]{:S(2)}, u32[]{:S(2)}) collective-permute-start(bf16[40,768]{1,0:T(8,128)(2,1)S(1)} %get-tuple-element.233), channel_id=1, source_target_pairs={{0,4},{4,0},{8,12},{12,8},{1,5},{5,1},{9,13},{13,9},{2,6},{6,2},{1... | collective-permute-start | bytes 184328 | tf_op jit(solution)/shard_map/ppermute | solution.py:33
  142.9 10.1 %collective-permute-start.57 = (bf16[40,768]{1,0:T(8,128)(2,1)S(1)}, bf16[40,768]{1,0:T(8,128)(2,1)S(1)}, u32[]{:S(2)}, u32[]{:S(2)}) collective-permute-start(bf16[40,768]{1,0:T(8,128)(2,1)S(1)} %get-tuple-element.234), channel_id=1, source_target_pairs={{0,8},{4,12},{8,0},{12,4},{1,9},{5,13},{9,1},{13,5},{2,10},{6,14},... | collective-permute-start | bytes 184328 | tf_op jit(solution)/shard_map/ppermute | solution.py:33
  145.5 7.5 %collective-permute-start.58 = (bf16[40,768]{1,0:T(8,128)(2,1)S(1)}, bf16[40,768]{1,0:T(8,128)(2,1)S(1)}, u32[]{:S(2)}, u32[]{:S(2)}) collective-permute-start(bf16[40,768]{1,0:T(8,128)(2,1)S(1)} %get-tuple-element.235), channel_id=1, source_target_pairs={{0,12},{4,8},{8,4},{12,0},{1,13},{5,9},{9,5},{13,1},{2,14},{6,10},... | collective-permute-start | bytes 184328 | tf_op jit(solution)/shard_map/ppermute | solution.py:33
  (42 other events, 233.1 us)

commit v2 on v1

--- a/solution.py
+++ b/solution.py
@@ -300,7 +300,8 @@
         rows += [sums[r : r + 1, :D], sums[r : r + 1, D:]]
     vec = taken(jnp.concatenate(rows, axis=0), n)
     gain[0] = vec[:2]
-    bias[0] = vec[2:]
+    for r in range(6):
+        bias[r] = vec[2 + r : 3 + r]
     both = jnp.concatenate([sums[4:5], sums[5:6]], axis=1)
     up_vec[...] = taken(jnp.broadcast_to(both, (8, FF)), 4 * n)[:1]
 
@@ -351,7 +352,7 @@
     keys = k_ref.shape[0]
     start = jnp.zeros((1, rows), F32)
     worst = lax.fori_loop(
-        0, HEADS // 2, functools.partial(one_pair, keys // 4), start, unroll=True
+        0, HEADS // 2, functools.partial(one_pair, keys // 8), start, unroll=True
     )
 
     @pl.when(jnp.max(worst) > LARGEST_SUM)
@@ -966,7 +967,7 @@
             sds((1, n, FF), F32),
             sds((1, 4 * n, D), F32),
             sds((1, 2, n), F32),
-            sds((1, 6, n), F32),
+            sds((6, 1, n), F32),
             sds((1, 4 * n), F32),
         ],
         [ids, *shares[0], shares[1], got],
@@ -981,7 +982,7 @@
         up_grad,
         down_grad,
         gain,
-        bias,
+        bias.transpose(1, 0, 2),
         up_vec,
     )
 

time: 163 us -> 162 us (level)
    unnamed x30 -> x29, local copies, waits for them, and re-layouts: 5.42 us -> 4.84 us
where the time goes in v2:
time: 162 us
  waiting for transfers between devices  53 us (33%)
  starting transfers between devices  52.6 us (32%)
  Pallas kernels  50 us (31%)
  local copies, waits for them, and re-layouts  4.84 us (3%)
    pallas_call x31, Pallas kernels, call(): pl.pallas_call(body, out_shape=outs, in_specs=[smem] * scalars + [vmem] *...  50 us
    ppermute x51, waiting for transfers between devices, xor_pass(): return lax.ppermute(x, axis, pairs)  46.5 us
    ppermute x51, starting transfers between devices, xor_pass(): return lax.ppermute(x, axis, pairs)  39.4 us
    unnamed x29, local copies, waits for them, and re-layouts  4.84 us
    ppermute x2, starting transfers between devices, from_clip(): lax.ppermute(swap, both, pairs(1))  4.69 us
  transfers between devices with their start and end apart: 60, of which 28 were waited for; matrix products, arithmetic and copies ran while one was open for 0% of the time, Pallas kernels for 23%

profile of v2, /device:TPU:0, one launch (start us, length us, event | category | flops | bytes accessed | tf_op | source)
XLA Modules:
  0.0 161.9 jit_solution(5616567128535336678)
XLA Ops:
  3.4 3.0 %collective-permute-start = (bf16[2,256,384]{2,1,0:T(8,128)(2,1)S(1)}, bf16[2,256,384]{2,1,0:T(8,128)(2,1)S(1)}, u32[]{:S(2)}, u32[]{:S(2)}) collective-permute-start(bf16[2,256,384]{2,1,0:T(8,128)(2,1)S(1)} %get-tuple-element.126.refs_3_.refs_4_), channel_id=1, source_target_pairs={{0,1},{1,0},{2,3},{3,2},{16,18},{17,19},{18,16},{19,17},{4,5},{5,4... | collective-permute-start | bytes 1179656 | tf_op jit(solution)/shard_map/ppermute | solution.py:637
  7.9 1.9 %collective-permute-start.2 = (bf16[96,1152]{1,0:T(8,128)(2,1)}, bf16[96,1152]{1,0:T(8,128)(2,1)S(1)}, u32[]{:S(2)}, u32[]{:S(2)}) collective-permute-start(bf16[96,1152]{1,0:T(8,128)(2,1)} %bitcast.31), channel_id=1, source_target_pairs={{0,1},{1,0},{2,3},{3,2},{4,5},{5,4},{6,7},{7,6},{8,9},{9,8},{10,11... | collective-permute-start | bytes 663560 | tf_op jit(solution)/shard_map/ppermute | solution.py:33
  15.0 10.2 %collective-permute-done.1.refs_1_ = bf16[128,384]{1,0:T(8,128)(2,1)S(1)} collective-permute-done((bf16[128,384]{1,0:T(8,128)(2,1)S(1)}, bf16[128,384]{1,0:T(8,128)(2,1)S(1)}, u32[]{:S(2)}, u32[]{:S(2)}) %collective-permute-start.1) | collective-permute-done | bytes 98336 | tf_op jit(solution)/shard_map/ppermute | solution.py:33
  27.4 1.5 collective-permute-start.15
  29.0 1.5 collective-permute-start.14
  34.4 5.0 %attend.2 = (bf16[384,1152]{1,0:T(8,128)(2,1)S(1)}, bf16[1024,384]{1,0:T(8,128)(2,1)S(1)}, bf16[256,384]{1,0:T(8,128)(2,1)S(1)}, bf16[1024,384]{1,0:T(8,128)(2,1...) custom-call(s32[4]{0:T(128)S(1)} %pad_add_fusion.refs_0_, ...), custom_call_target="tpu_custom_call" | custom-call | flops 4000000 | bytes 6225 | tf_op jit(solution)/shard_map/attend/pallas_call | solution.py:47
  39.4 5.9 %collective-permute-done.14.refs_1_ = bf16[48,3456]{1,0:T(8,128)(2,1)S(1)} collective-permute-done((bf16[48,3456]{1,0:T(8,128)(2,1)S(1)}, bf16[48,3456]{1,0:T(8,128)(2,1)S(1)}, u32[]{:S(2)}, u32[]{:S(2)}) %collective-permute-start.14) | collective-permute-done | bytes 331808 | tf_op jit(solution)/shard_map/ppermute | solution.py:33
  47.9 2.5 %mlp.2 = (bf16[256,384]{1,0:T(8,128)(2,1)S(1)}, f32[256,384]{1,0:T(8,128)S(1)}, bf16[256,1536]{1,0:T(8,128)(2,1)S(1)}, bf16[256,1536]{1,0:T(8,128)(2,1)S(1)}, bf...) custom-call(s32[4]{0:T(128)S(1)} %pad_add_fusion.refs_0_, ...), custom_call_target="tpu_custom_call" | custom-call | flops 2000000 | bytes 7888 | tf_op jit(solution)/shard_map/mlp/pallas_call | solution.py:47
  53.0 4.4 %collective-permute-done.21.refs_3_.refs_2_ = bf16[256,384]{1,0:T(8,128)(2,1)S(1)} collective-permute-done((bf16[256,384]{1,0:T(8,128)(2,1)S(1)}, bf16[256,384]{1,0:T(8,128)(2,1)S(1)}, u32[]{:S(2)}, u32[]{:S(2)}) %collective-permute-start.21) | collective-permute-done | bytes 196640 | tf_op jit(solution)/shard_map/ppermute | solution.py:33
  60.8 5.0 %attend.3 = (bf16[384,1152]{1,0:T(8,128)(2,1)S(1)}, bf16[1024,384]{1,0:T(8,128)(2,1)S(1)}, bf16[256,384]{1,0:T(8,128)(2,1)S(1)}, bf16[1024,384]{1,0:T(8,128)(2,1...) custom-call(s32[4]{0:T(128)S(1)} %pad_add_fusion.refs_0_, ...), custom_call_target="tpu_custom_call" | custom-call | flops 4000000 | bytes 6225 | tf_op jit(solution)/shard_map/attend/pallas_call | solution.py:47
  65.9 2.4 %collective-permute-done.26.refs_0_ = bf16[2,48,3456]{2,1,0:T(8,128)(2,1)S(1)} collective-permute-done((bf16[2,48,3456]{2,1,0:T(8,128)(2,1)S(1)}, bf16[2,48,3456]{2,1,0:T(8,128)(2,1)S(1)}, u32[]{:S(2)}, u32[]{:S(2)}) %collective-permute-start.26) | collective-permute-done | bytes 663584 | tf_op jit(solution)/shard_map/ppermute | solution.py:619
  68.2 2.1 %collective-permute-done.27.refs_9_ = bf16[2,48,3456]{2,1,0:T(8,128)(2,1)S(1)} collective-permute-done((bf16[2,48,3456]{2,1,0:T(8,128)(2,1)S(1)}, bf16[2,48,3456]{2,1,0:T(8,128)(2,1)S(1)}, u32[]{:S(2)}, u32[]{:S(2)}) %collective-permute-start.27) | collective-permute-done | bytes 663584 | tf_op jit(solution)/shard_map/ppermute | solution.py:33
  70.3 2.5 %mlp.3 = (bf16[256,384]{1,0:T(8,128)(2,1)S(1)}, f32[256,384]{1,0:T(8,128)S(1)}, bf16[256,1536]{1,0:T(8,128)(2,1)S(1)}, bf16[256,1536]{1,0:T(8,128)(2,1)S(1)}, bf...) custom-call(s32[4]{0:T(128)S(1)} %pad_add_fusion.refs_0_, ...), custom_call_target="tpu_custom_call" | custom-call | flops 2000000 | bytes 7888 | tf_op jit(solution)/shard_map/mlp/pallas_call | solution.py:47
  74.3 6.0 %attend_back.2 = (f32[256,384]{1,0:T(8,128)S(1)}, f32[256,384]{1,0:T(8,128)S(1)}, bf16[2,256,384]{2,1,0:T(8,128)(2,1)S(1)}, bf16[256,384]{1,0:T(8,128)(2,1)S(1)}...) custom-call(bf16[256,384]{1,0:T(8,128)(2,1)S(1)} %get-tuple-element.151.refs_0_, ...), custom_call_target="tpu_custom_call" | custom-call | flops 8000000 | bytes 6803 | tf_op jit(solution)/shard_map/attend_back/pallas_call | solution.py:47
  80.5 1.6 collective-permute-done.28.refs_1_
  83.4 3.7 %grad.2 = (bf16[4,304,768]{2,1,0:T(8,128)(2,1)S(1)}, bf16[2,304,768]{2,1,0:T(8,128)(2,1)S(1)}, bf16[2,304,768]{2,1,0:T(8,128)(2,1)S(1)}) custom-call(s32[4]{0:T(128)S(1)} %pad_add_fusion.refs_0_, bf16[256,384]{1,0:T(8,128)(2,1)S(1)} %get-tuple-element.178.refs_1_, bf16[256,1536]{1,0:T(8,128)(2,1)S(1)} %get-tuple-element.179.refs_2_, ...), custom_call_target="tpu_custom_call" | custom-call | flops 4000000 | bytes 8706 | tf_op jit(solution)/shard_map/grad/pallas_call | solution.py:47
  87.0 2.1 %collective-permute-done.29.refs_2_ = bf16[256,384]{1,0:T(8,128)(2,1)S(1)} collective-permute-done((bf16[256,384]{1,0:T(8,128)(2,1)S(1)}, bf16[256,384]{1,0:T(8,128)(2,1)S(1)}, u32[]{:S(2)}, u32[]{:S(2)}) %collective-permute-start.29) | collective-permute-done | bytes 196640 | tf_op jit(solution)/shard_map/ppermute | solution.py:33
  89.6 2.0 %collective-permute-done.30.refs_1_ = bf16[2,304,768]{2,1,0:T(8,128)(2,1)S(1)} collective-permute-done((bf16[2,304,768]{2,1,0:T(8,128)(2,1)S(1)}, bf16[2,304,768]{2,1,0:T(8,128)(2,1)S(1)}, u32[]{:S(2)}, u32[]{:S(2)}) %collective-permute-start.30) | collective-permute-done | bytes 933920 | tf_op jit(solution)/shard_map/ppermute | solution.py:33
  96.5 5.9 %attend_back.3 = (f32[256,384]{1,0:T(8,128)S(1)}, f32[256,384]{1,0:T(8,128)S(1)}, bf16[2,256,384]{2,1,0:T(8,128)(2,1)S(1)}, bf16[256,384]{1,0:T(8,128)(2,1)S(1)}...) custom-call(bf16[256,384]{1,0:T(8,128)(2,1)S(1)} %get-tuple-element.147.refs_0_, ...), custom_call_target="tpu_custom_call" | custom-call | flops 8000000 | bytes 6803 | tf_op jit(solution)/shard_map/attend_back/pallas_call | solution.py:47
  103.8 2.3 %collective-permute-start.33 = (bf16[256,384]{1,0:T(8,128)(2,1)S(1)}, bf16[256,384]{1,0:T(8,128)(2,1)S(1)}, u32[]{:S(2)}, u32[]{:S(2)}) collective-permute-start(bf16[256,384]{1,0:T(8,128)(2,1)S(1)} %get-tuple-element.194), channel_id=1, source_target_pairs={{0,16},{1,17},{2,0},{3,1},{16,18},{17,19},{18,2},{19,3},{4,20},{5,... | collective-permute-start | bytes 589832 | tf_op jit(solution)/shard_map/ppermute | solution.py:667
  107.1 3.4 %grad.3 = (bf16[4,192,768]{2,1,0:T(8,128)(2,1)S(1)}, bf16[2,192,768]{2,1,0:T(8,128)(2,1)S(1)}, bf16[2,192,768]{2,1,0:T(8,128)(2,1)S(1)}, bf16[4,112,768]{2,1,0:T...) custom-call(s32[4]{0:T(128)S(1)} %pad_add_fusion.refs_0_, ...), custom_call_target="tpu_custom_call" | custom-call | flops 4000000 | bytes 8706 | tf_op jit(solution)/shard_map/grad/pallas_call | solution.py:47
  115.2 2.4 %collective-permute-start.37 = (bf16[256,384]{1,0:T(8,128)(2,1)S(1)}, bf16[256,384]{1,0:T(8,128)(2,1)S(1)}, u32[]{:S(2)}, u32[]{:S(2)}) collective-permute-start(bf16[256,384]{1,0:T(8,128)(2,1)S(1)} %get-tuple-element.199), channel_id=1, source_target_pairs={{0,16},{1,17},{2,0},{3,1},{16,18},{17,19},{18,2},{19,3},{4,20},{5,... | collective-permute-start | bytes 589832 | tf_op jit(solution)/shard_map/ppermute | solution.py:667
  117.6 2.2 %collective-permute-done.43.refs_7_.refs_3_ = bf16[304,768]{1,0:T(8,128)(2,1)S(1)} collective-permute-done((bf16[304,768]{1,0:T(8,128)(2,1)S(1)}, bf16[304,768]{1,0:T(8,128)(2,1)S(1)}, u32[]{:S(2)}, u32[]{:S(2)}) %collective-permute-start.43) | collective-permute-done | bytes 466976 | tf_op jit(solution)/shard_map/ppermute | solution.py:719
  123.2 1.6 %collective-permute-start.47 = (bf16[88,768]{1,0:T(8,128)(2,1)S(1)}, bf16[88,768]{1,0:T(8,128)(2,1)S(1)}, u32[]{:S(2)}, u32[]{:S(2)}) collective-permute-start(bf16[88,768]{1,0:T(8,128)(2,1)S(1)} %get-tuple-element.221), channel_id=1, source_target_pairs={{0,4},{4,0},{8,12},{12,8},{1,5},{5,1},{9,13},{13,9},{2,6},{6,2},{1... | collective-permute-start | bytes 405512 | tf_op jit(solution)/shard_map/ppermute | solution.py:33
  128.3 2.6 %collective-permute-start.48 = (bf16[88,768]{1,0:T(8,128)(2,1)S(1)}, bf16[88,768]{1,0:T(8,128)(2,1)S(1)}, u32[]{:S(2)}, u32[]{:S(2)}) collective-permute-start(bf16[88,768]{1,0:T(8,128)(2,1)S(1)} %get-tuple-element.222), channel_id=1, source_target_pairs={{0,8},{4,12},{8,0},{12,4},{1,9},{5,13},{9,1},{13,5},{2,10},{6,14},... | collective-permute-start | bytes 405512 | tf_op jit(solution)/shard_map/ppermute | solution.py:33
  133.6 2.8 %collective-permute-done.55.refs_4_ = bf16[112,768]{1,0:T(8,128)(2,1)S(1)} collective-permute-done((bf16[112,768]{1,0:T(8,128)(2,1)S(1)}, bf16[112,768]{1,0:T(8,128)(2,1)S(1)}, u32[]{:S(2)}, u32[]{:S(2)}) %collective-permute-start.55) | collective-permute-done | bytes 172064 | tf_op jit(solution)/shard_map/ppermute | solution.py:33
  141.3 1.7 %collective-permute-start.56 = (bf16[40,768]{1,0:T(8,128)(2,1)S(1)}, bf16[40,768]{1,0:T(8,128)(2,1)S(1)}, u32[]{:S(2)}, u32[]{:S(2)}) collective-permute-start(bf16[40,768]{1,0:T(8,128)(2,1)S(1)} %get-tuple-element.233), channel_id=1, source_target_pairs={{0,4},{4,0},{8,12},{12,8},{1,5},{5,1},{9,13},{13,9},{2,6},{6,2},{1... | collective-permute-start | bytes 184328 | tf_op jit(solution)/shard_map/ppermute | solution.py:33
  142.9 2.6 %collective-permute-start.57 = (bf16[40,768]{1,0:T(8,128)(2,1)S(1)}, bf16[40,768]{1,0:T(8,128)(2,1)S(1)}, u32[]{:S(2)}, u32[]{:S(2)}) collective-permute-start(bf16[40,768]{1,0:T(8,128)(2,1)S(1)} %get-tuple-element.234), channel_id=1, source_target_pairs={{0,8},{4,12},{8,0},{12,4},{1,9},{5,13},{9,1},{13,5},{2,10},{6,14},... | collective-permute-start | bytes 184328 | tf_op jit(solution)/shard_map/ppermute | solution.py:33
  145.8 1.9 %collective-permute-done.45.refs_3_ = bf16[192,768]{1,0:T(8,128)(2,1)S(1)} collective-permute-done((bf16[192,768]{1,0:T(8,128)(2,1)S(1)}, bf16[192,768]{1,0:T(8,128)(2,1)S(1)}, u32[]{:S(2)}, u32[]{:S(2)}) %collective-permute-start.45) | collective-permute-done | bytes 294944 | tf_op jit(solution)/shard_map/ppermute | solution.py:33
  149.7 2.5 %collective-permute-start.51 = (bf16[48,768]{1,0:T(8,128)(2,1)S(1)}, bf16[48,768]{1,0:T(8,128)(2,1)S(1)}, u32[]{:S(2)}, u32[]{:S(2)}) collective-permute-start(bf16[48,768]{1,0:T(8,128)(2,1)S(1)} %get-tuple-element.226), channel_id=1, source_target_pairs={{0,8},{4,12},{8,0},{12,4},{1,9},{5,13},{9,1},{13,5},{2,10},{6,14},... | collective-permute-start | bytes 221192 | tf_op jit(solution)/shard_map/ppermute | solution.py:33
  153.2 3.2 %collective-permute-done.51 = bf16[48,768]{1,0:T(8,128)(2,1)S(1)} collective-permute-done((bf16[48,768]{1,0:T(8,128)(2,1)S(1)}, bf16[48,768]{1,0:T(8,128)(2,1)S(1)}, u32[]{:S(2)}, u32[]{:S(2)}) %collective-permute-start.51) | collective-permute-done | bytes 73760 | tf_op jit(solution)/shard_map/ppermute | solution.py:33
  156.5 1.9 %collective-permute-done.52 = bf16[48,768]{1,0:T(8,128)(2,1)S(1)} collective-permute-done((bf16[48,768]{1,0:T(8,128)(2,1)S(1)}, bf16[48,768]{1,0:T(8,128)(2,1)S(1)}, u32[]{:S(2)}, u32[]{:S(2)}) %collective-permute-start.52) | collective-permute-done | bytes 73760 | tf_op jit(solution)/shard_map/ppermute | solution.py:33
  (159 shorter events, 60.4 us)
Async XLA Ops:
  3.4 21.9 %collective-permute-start = (bf16[2,256,384]{2,1,0:T(8,128)(2,1)S(1)}, bf16[2,256,384]{2,1,0:T(8,128)(2,1)S(1)}, u32[]{:S(2)}, u32[]{:S(2)}) collective-permute-start(bf16[2,256,384]{2,1,0:T(8,128)(2,1)S(1)} %get-tuple-element.126.refs_3_.refs_4_), channel_id=1, source_target_pairs={{0,1},{1,0},{2,3},{3,2},{16,18},{17,19},{18,16},{19,17},{4,5},{5,4... | collective-permute-start | bytes 1179656 | tf_op jit(solution)/shard_map/ppermute | solution.py:637
  6.4 18.8 %collective-permute-start.4 = (bf16[96,1152]{1,0:T(8,128)(2,1)}, bf16[96,1152]{1,0:T(8,128)(2,1)S(1)}, u32[]{:S(2)}, u32[]{:S(2)}) collective-permute-start(bf16[96,1152]{1,0:T(8,128)(2,1)} %bitcast.29), channel_id=1, source_target_pairs={{0,3},{1,2},{2,1},{3,0},{4,7},{5,6},{6,5},{7,4},{8,11},{9,10},{10,... | collective-permute-start | bytes 663560 | tf_op jit(solution)/shard_map/ppermute | solution.py:33
  7.9 17.4 %collective-permute-start.3 = (bf16[96,1152]{1,0:T(8,128)(2,1)}, bf16[96,1152]{1,0:T(8,128)(2,1)S(1)}, u32[]{:S(2)}, u32[]{:S(2)}) collective-permute-start(bf16[96,1152]{1,0:T(8,128)(2,1)} %bitcast.30), channel_id=1, source_target_pairs={{0,2},{1,3},{2,0},{3,1},{4,6},{5,7},{6,4},{7,5},{8,10},{9,11},{10,... | collective-permute-start | bytes 663560 | tf_op jit(solution)/shard_map/ppermute | solution.py:33
  7.9 17.3 %collective-permute-start.2 = (bf16[96,1152]{1,0:T(8,128)(2,1)}, bf16[96,1152]{1,0:T(8,128)(2,1)S(1)}, u32[]{:S(2)}, u32[]{:S(2)}) collective-permute-start(bf16[96,1152]{1,0:T(8,128)(2,1)} %bitcast.31), channel_id=1, source_target_pairs={{0,1},{1,0},{2,3},{3,2},{4,5},{5,4},{6,7},{7,6},{8,9},{9,8},{10,11... | collective-permute-start | bytes 663560 | tf_op jit(solution)/shard_map/ppermute | solution.py:33
  9.9 15.3 %collective-permute-start.1 = (bf16[128,384]{1,0:T(8,128)(2,1)S(1)}, bf16[128,384]{1,0:T(8,128)(2,1)S(1)}, u32[]{:S(2)}, u32[]{:S(2)}) collective-permute-start(bf16[128,384]{1,0:T(8,128)(2,1)S(1)} %get-tuple-element.127), channel_id=1, source_target_pairs={{0,3},{1,2},{2,1},{3,0},{4,7},{5,6},{6,5},{7,4},{8,11},{9,10},{10,... | collective-permute-start | bytes 294920 | tf_op jit(solution)/shard_map/ppermute | solution.py:33
  25.3 7.2 %collective-permute-start.5 = (bf16[2,256,384]{2,1,0:T(8,128)(2,1)S(1)}, bf16[2,256,384]{2,1,0:T(8,128)(2,1)S(1)}, u32[]{:S(2)}, u32[]{:S(2)}) collective-permute-start(bf16[2,256,384]{2,1,0:T(8,128)(2,1)S(1)} %get-tuple-element.128.refs_4_), channel_id=1, source_target_pairs={{0,16},{16,0},{1,17},{17,1},{2,18},{18,2},{3,19},{19,3},{4,20},{20... | collective-permute-start | bytes 1179656 | tf_op jit(solution)/shard_map/ppermute | solution.py:33
  27.4 12.0 %collective-permute-start.15 = (bf16[48,3456]{1,0:T(8,128)(2,1)S(1)}, bf16[48,3456]{1,0:T(8,128)(2,1)S(1)}, u32[]{:S(2)}, u32[]{:S(2)}) collective-permute-start(bf16[48,3456]{1,0:T(8,128)(2,1)S(1)} %get-tuple-element.138.refs_4_), channel_id=1, source_target_pairs={{0,3},{1,2},{2,1},{3,0},{4,7},{5,6},{6,5},{7,4},{8,11},{9,10},{10,... | collective-permute-start | bytes 995336 | tf_op jit(solution)/shard_map/ppermute | solution.py:33
  29.0 16.4 %collective-permute-start.14 = (bf16[48,3456]{1,0:T(8,128)(2,1)S(1)}, bf16[48,3456]{1,0:T(8,128)(2,1)S(1)}, u32[]{:S(2)}, u32[]{:S(2)}) collective-permute-start(bf16[48,3456]{1,0:T(8,128)(2,1)S(1)} %get-tuple-element.138.refs_4_), channel_id=1, source_target_pairs={{0,2},{1,3},{2,0},{3,1},{4,6},{5,7},{6,4},{7,5},{8,10},{9,11},{10,... | collective-permute-start | bytes 995336 | tf_op jit(solution)/shard_map/ppermute | solution.py:33
  30.5 14.8 %collective-permute-start.13 = (bf16[48,3456]{1,0:T(8,128)(2,1)S(1)}, bf16[48,3456]{1,0:T(8,128)(2,1)S(1)}, u32[]{:S(2)}, u32[]{:S(2)}) collective-permute-start(bf16[48,3456]{1,0:T(8,128)(2,1)S(1)} %get-tuple-element.138.refs_4_), channel_id=1, source_target_pairs={{0,1},{1,0},{2,3},{3,2},{4,5},{5,4},{6,7},{7,6},{8,9},{9,8},{10,11... | collective-permute-start | bytes 995336 | tf_op jit(solution)/shard_map/ppermute | solution.py:33
  34.2 12.9 %collective-permute-start.16 = (bf16[48,3456]{1,0:T(8,128)(2,1)S(1)}, bf16[48,3456]{1,0:T(8,128)(2,1)S(1)}, u32[]{:S(2)}, u32[]{:S(2)}) collective-permute-start(bf16[48,3456]{1,0:T(8,128)(2,1)S(1)} %get-tuple-element.138.refs_4_), channel_id=1, source_target_pairs={{0,16},{16,0},{1,17},{17,1},{2,18},{18,2},{3,19},{19,3},{4,20},{20... | collective-permute-start | bytes 995336 | tf_op jit(solution)/shard_map/ppermute | solution.py:33
  45.9 7.1 %collective-permute-start.24 = (bf16[48,3456]{1,0:T(8,128)(2,1)S(1)}, bf16[48,3456]{1,0:T(8,128)(2,1)S(1)}, u32[]{:S(2)}, u32[]{:S(2)}) collective-permute-start(bf16[48,3456]{1,0:T(8,128)(2,1)S(1)} %after.7.refs_0_.refs_4_), channel_id=1, source_target_pairs={{0,1},{1,0},{2,3},{3,2},{16,18},{17,19},{18,16},{19,17},{4,5},{5,4... | collective-permute-start | bytes 995336 | tf_op jit(solution)/shard_map/ppermute | solution.py:606
  50.4 7.0 %collective-permute-start.21 = (bf16[256,384]{1,0:T(8,128)(2,1)S(1)}, bf16[256,384]{1,0:T(8,128)(2,1)S(1)}, u32[]{:S(2)}, u32[]{:S(2)}) collective-permute-start(bf16[256,384]{1,0:T(8,128)(2,1)S(1)} %get-tuple-element.142.refs_1_.refs_2_.refs_3_), channel_id=1, source_target_pairs={{0,1},{1,0},{2,3},{3,2},{4,5},{5,4},{6,7},{7,6},{8,9},{9,8},{10,11... | collective-permute-start | bytes 589832 | tf_op jit(solution)/shard_map/ppermute | solution.py:33
  57.5 10.7 %collective-permute-start.26 = (bf16[2,48,3456]{2,1,0:T(8,128)(2,1)S(1)}, bf16[2,48,3456]{2,1,0:T(8,128)(2,1)S(1)}, u32[]{:S(2)}, u32[]{:S(2)}) collective-permute-start(bf16[2,48,3456]{2,1,0:T(8,128)(2,1)S(1)} %stack.21), channel_id=1, source_target_pairs={{0,2},{1,3},{2,0},{3,1},{16,17},{17,16},{18,19},{19,18},{4,6},{5,7... | collective-permute-start | bytes 1990664 | tf_op jit(solution)/shard_map/ppermute | solution.py:619
  82.1 7.0 %collective-permute-start.29 = (bf16[256,384]{1,0:T(8,128)(2,1)S(1)}, bf16[256,384]{1,0:T(8,128)(2,1)S(1)}, u32[]{:S(2)}, u32[]{:S(2)}) collective-permute-start(bf16[256,384]{1,0:T(8,128)(2,1)S(1)} %fusion.1.refs_14_), channel_id=1, source_target_pairs={{0,1},{1,0},{2,3},{3,2},{4,5},{5,4},{6,7},{7,6},{8,9},{9,8},{10,11... | collective-permute-start | bytes 589832 | tf_op jit(solution)/shard_map/ppermute | solution.py:33
  93.4 17.2 %collective-permute-start.42 = (bf16[2,304,768]{2,1,0:T(8,128)(2,1)S(1)}, bf16[2,304,768]{2,1,0:T(8,128)(2,1)S(1)}, u32[]{:S(2)}, u32[]{:S(2)}) collective-permute-start(bf16[2,304,768]{2,1,0:T(8,128)(2,1)S(1)} %get-tuple-element.191.refs_8_), channel_id=1, source_target_pairs={{0,1},{1,0},{2,3},{3,2},{16,18},{17,19},{18,16},{19,17},{4,5},{5,4... | collective-permute-start | bytes 2801672 | tf_op jit(solution)/shard_map/ppermute | solution.py:706
  103.1 8.1 %collective-permute-start.32 = (bf16[256,384]{1,0:T(8,128)(2,1)S(1)}, bf16[256,384]{1,0:T(8,128)(2,1)S(1)}, u32[]{:S(2)}, u32[]{:S(2)}) collective-permute-start(bf16[256,384]{1,0:T(8,128)(2,1)S(1)} %get-tuple-element.193), channel_id=1, source_target_pairs={{0,0},{1,1},{2,16},{3,17},{16,2},{17,3},{18,18},{19,19},{4,4},{5,5... | collective-permute-start | bytes 589832 | tf_op jit(solution)/shard_map/ppermute | solution.py:667
  103.8 9.1 %collective-permute-start.33 = (bf16[256,384]{1,0:T(8,128)(2,1)S(1)}, bf16[256,384]{1,0:T(8,128)(2,1)S(1)}, u32[]{:S(2)}, u32[]{:S(2)}) collective-permute-start(bf16[256,384]{1,0:T(8,128)(2,1)S(1)} %get-tuple-element.194), channel_id=1, source_target_pairs={{0,16},{1,17},{2,0},{3,1},{16,18},{17,19},{18,2},{19,3},{4,20},{5,... | collective-permute-start | bytes 589832 | tf_op jit(solution)/shard_map/ppermute | solution.py:667
  110.5 7.1 %collective-permute-start.38 = (bf16[2,192,768]{2,1,0:T(8,128)(2,1)S(1)}, bf16[2,192,768]{2,1,0:T(8,128)(2,1)S(1)}, u32[]{:S(2)}, u32[]{:S(2)}) collective-permute-start(bf16[2,192,768]{2,1,0:T(8,128)(2,1)S(1)} %get-tuple-element.209), channel_id=1, source_target_pairs={{0,16},{16,0},{1,17},{17,1},{2,18},{18,2},{3,19},{19,3},{4,20},{20... | collective-permute-start | bytes 1769480 | tf_op jit(solution)/shard_map/ppermute | solution.py:33
  111.2 8.6 %collective-permute-start.43 = (bf16[304,768]{1,0:T(8,128)(2,1)S(1)}, bf16[304,768]{1,0:T(8,128)(2,1)S(1)}, u32[]{:S(2)}, u32[]{:S(2)}) collective-permute-start(bf16[304,768]{1,0:T(8,128)(2,1)S(1)} %second.1), channel_id=1, source_target_pairs={{0,2},{1,3},{2,0},{3,1},{16,17},{17,16},{18,19},{19,18},{4,6},{5,7... | collective-permute-start | bytes 1400840 | tf_op jit(solution)/shard_map/ppermute | solution.py:719
  114.5 10.4 %collective-permute-start.36 = (bf16[256,384]{1,0:T(8,128)(2,1)S(1)}, bf16[256,384]{1,0:T(8,128)(2,1)S(1)}, u32[]{:S(2)}, u32[]{:S(2)}) collective-permute-start(bf16[256,384]{1,0:T(8,128)(2,1)S(1)} %get-tuple-element.198), channel_id=1, source_target_pairs={{0,0},{1,1},{2,16},{3,17},{16,2},{17,3},{18,18},{19,19},{4,4},{5,5... | collective-permute-start | bytes 589832 | tf_op jit(solution)/shard_map/ppermute | solution.py:667
  115.2 11.1 %collective-permute-start.37 = (bf16[256,384]{1,0:T(8,128)(2,1)S(1)}, bf16[256,384]{1,0:T(8,128)(2,1)S(1)}, u32[]{:S(2)}, u32[]{:S(2)}) collective-permute-start(bf16[256,384]{1,0:T(8,128)(2,1)S(1)} %get-tuple-element.199), channel_id=1, source_target_pairs={{0,16},{1,17},{2,0},{3,1},{16,18},{17,19},{18,2},{19,3},{4,20},{5,... | collective-permute-start | bytes 589832 | tf_op jit(solution)/shard_map/ppermute | solution.py:667
  120.2 10.7 %collective-permute-start.53 = (bf16[112,768]{1,0:T(8,128)(2,1)S(1)}, bf16[112,768]{1,0:T(8,128)(2,1)S(1)}, u32[]{:S(2)}, u32[]{:S(2)}) collective-permute-start(bf16[112,768]{1,0:T(8,128)(2,1)S(1)} %get-tuple-element.229), channel_id=1, source_target_pairs={{0,1},{1,0},{2,3},{3,2},{4,5},{5,4},{6,7},{7,6},{8,9},{9,8},{10,11... | collective-permute-start | bytes 516104 | tf_op jit(solution)/shard_map/ppermute | solution.py:33
  121.4 24.1 %collective-permute-start.44 = (bf16[192,768]{1,0:T(8,128)(2,1)S(1)}, bf16[192,768]{1,0:T(8,128)(2,1)S(1)}, u32[]{:S(2)}, u32[]{:S(2)}) collective-permute-start(bf16[192,768]{1,0:T(8,128)(2,1)S(1)} %get-tuple-element.216), channel_id=1, source_target_pairs={{0,1},{1,0},{2,3},{3,2},{4,5},{5,4},{6,7},{7,6},{8,9},{9,8},{10,11... | collective-permute-start | bytes 884744 | tf_op jit(solution)/shard_map/ppermute | solution.py:33
  124.9 7.4 %collective-permute-start.54 = (bf16[112,768]{1,0:T(8,128)(2,1)S(1)}, bf16[112,768]{1,0:T(8,128)(2,1)S(1)}, u32[]{:S(2)}, u32[]{:S(2)}) collective-permute-start(bf16[112,768]{1,0:T(8,128)(2,1)S(1)} %get-tuple-element.230), channel_id=1, source_target_pairs={{0,2},{1,3},{2,0},{3,1},{4,6},{5,7},{6,4},{7,5},{8,10},{9,11},{10,... | collective-permute-start | bytes 516104 | tf_op jit(solution)/shard_map/ppermute | solution.py:33
  126.3 10.2 %collective-permute-start.55 = (bf16[112,768]{1,0:T(8,128)(2,1)S(1)}, bf16[112,768]{1,0:T(8,128)(2,1)S(1)}, u32[]{:S(2)}, u32[]{:S(2)}) collective-permute-start(bf16[112,768]{1,0:T(8,128)(2,1)S(1)} %get-tuple-element.231), channel_id=1, source_target_pairs={{0,3},{1,2},{2,1},{3,0},{4,7},{5,6},{6,5},{7,4},{8,11},{9,10},{10,... | collective-permute-start | bytes 516104 | tf_op jit(solution)/shard_map/ppermute | solution.py:33
  128.3 13.0 %collective-permute-start.48 = (bf16[88,768]{1,0:T(8,128)(2,1)S(1)}, bf16[88,768]{1,0:T(8,128)(2,1)S(1)}, u32[]{:S(2)}, u32[]{:S(2)}) collective-permute-start(bf16[88,768]{1,0:T(8,128)(2,1)S(1)} %get-tuple-element.222), channel_id=1, source_target_pairs={{0,8},{4,12},{8,0},{12,4},{1,9},{5,13},{9,1},{13,5},{2,10},{6,14},... | collective-permute-start | bytes 405512 | tf_op jit(solution)/shard_map/ppermute | solution.py:33
  130.9 12.1 %collective-permute-start.49 = (bf16[88,768]{1,0:T(8,128)(2,1)S(1)}, bf16[88,768]{1,0:T(8,128)(2,1)S(1)}, u32[]{:S(2)}, u32[]{:S(2)}) collective-permute-start(bf16[88,768]{1,0:T(8,128)(2,1)S(1)} %get-tuple-element.223), channel_id=1, source_target_pairs={{0,12},{4,8},{8,4},{12,0},{1,13},{5,9},{9,5},{13,1},{2,14},{6,10},... | collective-permute-start | bytes 405512 | tf_op jit(solution)/shard_map/ppermute | solution.py:33
  132.2 15.5 %collective-permute-start.45 = (bf16[192,768]{1,0:T(8,128)(2,1)S(1)}, bf16[192,768]{1,0:T(8,128)(2,1)S(1)}, u32[]{:S(2)}, u32[]{:S(2)}) collective-permute-start(bf16[192,768]{1,0:T(8,128)(2,1)S(1)} %get-tuple-element.217), channel_id=1, source_target_pairs={{0,2},{1,3},{2,0},{3,1},{4,6},{5,7},{6,4},{7,5},{8,10},{9,11},{10,... | collective-permute-start | bytes 884744 | tf_op jit(solution)/shard_map/ppermute | solution.py:33
  136.5 11.2 %collective-permute-start.46 = (bf16[192,768]{1,0:T(8,128)(2,1)S(1)}, bf16[192,768]{1,0:T(8,128)(2,1)S(1)}, u32[]{:S(2)}, u32[]{:S(2)}) collective-permute-start(bf16[192,768]{1,0:T(8,128)(2,1)S(1)} %get-tuple-element.218), channel_id=1, source_target_pairs={{0,3},{1,2},{2,1},{3,0},{4,7},{5,6},{6,5},{7,4},{8,11},{9,10},{10,... | collective-permute-start | bytes 884744 | tf_op jit(solution)/shard_map/ppermute | solution.py:33
  141.3 10.9 %collective-permute-start.56 = (bf16[40,768]{1,0:T(8,128)(2,1)S(1)}, bf16[40,768]{1,0:T(8,128)(2,1)S(1)}, u32[]{:S(2)}, u32[]{:S(2)}) collective-permute-start(bf16[40,768]{1,0:T(8,128)(2,1)S(1)} %get-tuple-element.233), channel_id=1, source_target_pairs={{0,4},{4,0},{8,12},{12,8},{1,5},{5,1},{9,13},{13,9},{2,6},{6,2},{1... | collective-permute-start | bytes 184328 | tf_op jit(solution)/shard_map/ppermute | solution.py:33
  142.9 10.1 %collective-permute-start.57 = (bf16[40,768]{1,0:T(8,128)(2,1)S(1)}, bf16[40,768]{1,0:T(8,128)(2,1)S(1)}, u32[]{:S(2)}, u32[]{:S(2)}) collective-permute-start(bf16[40,768]{1,0:T(8,128)(2,1)S(1)} %get-tuple-element.234), channel_id=1, source_target_pairs={{0,8},{4,12},{8,0},{12,4},{1,9},{5,13},{9,1},{13,5},{2,10},{6,14},... | collective-permute-start | bytes 184328 | tf_op jit(solution)/shard_map/ppermute | solution.py:33
  145.5 7.5 %collective-permute-start.58 = (bf16[40,768]{1,0:T(8,128)(2,1)S(1)}, bf16[40,768]{1,0:T(8,128)(2,1)S(1)}, u32[]{:S(2)}, u32[]{:S(2)}) collective-permute-start(bf16[40,768]{1,0:T(8,128)(2,1)S(1)} %get-tuple-element.235), channel_id=1, source_target_pairs={{0,12},{4,8},{8,4},{12,0},{1,13},{5,9},{9,5},{13,1},{2,14},{6,10},... | collective-permute-start | bytes 184328 | tf_op jit(solution)/shard_map/ppermute | solution.py:33
  (42 other events, 233.1 us)
